TPU v7x, 32 devices: a whole 2x2x4 slice. The times are simulated.
32 devices in a mesh: dp: 8 (over y, x, core), seq: 4 (over z).
Axes of the slice: x: 2, y: 2, z: 4, core: 2. Of those that a mesh axis runs over, the one named last changes fastest.
Arguments:
- dec_in: bfloat16 [24, 128, 1024], P('dp', 'seq'), may hold values from -6 to 6
- memory: bfloat16 [24, 7, 128, 1024], P('dp', None, 'seq'), may hold values from -6 to 6
- proj_w: bfloat16 [6, 1024, 1024], P(None, ('dp', 'seq')), may hold values from -0.1875 to 0.1875
- out_w: bfloat16 [2, 1024, 1024], P(None, ('dp', 'seq')), may hold values from -1.25 to 1.25
- ffn_in: bfloat16 [1024, 4096], P(('dp', 'seq')), may hold values from -0.1875 to 0.1875
- ffn_out: bfloat16 [4096, 1024], P(('dp', 'seq')), may hold values from -0.09375 to 0.09375
- biases: float32 [6, 1024], replicated, may hold values from -2 to 2
- out_bias: float32 [1024], replicated, may hold values from -2 to 2
- ffn_bias: float32 [4096], replicated, may hold values from -2 to 2
- norm_gain: float32 [3, 1024], replicated, may hold values from 0.5 to 1.5
- norm_bias: float32 [3, 1024], replicated, may hold values from -2 to 2
- mem_len: int32 [24], replicated, may hold values from 4 to 896, as said below
- dec_len: int32 [24], replicated, may hold values from 64 to 128, as said below
- mem_seg: int32 [24, 7, 128], P('dp'), may hold values from 0 to 3, as said below
- dec_seg: int32 [24, 128], P('dp'), may hold values from 0 to 3, as said below
- cotangent: bfloat16 [24, 128, 1024], P('dp', 'seq'), may hold values from -6 to 6
Outputs:
- mixed: bfloat16 [24, 128, 1024], P('dp', 'seq')
- d_dec: float32 [24, 128, 1024], P('dp', 'seq')
- d_memory: bfloat16 [24, 7, 128, 1024], P('dp', None, 'seq')
- g_proj: float32 [6, 1024, 1024], P(None, 'seq')
- g_out: float32 [2, 1024, 1024], P(None, 'seq')
- g_ffn_in: float32 [1024, 4096], P('seq')
- g_ffn_out: float32 [4096, 1024], P('seq')
- g_biases: float32 [6, 1024], P(None, 'seq')
- g_out_bias: float32 [1024], P('seq')
- g_ffn_bias: float32 [4096], P('seq')
- g_gain: float32 [3, 1024], P(None, 'seq')
- g_shift: float32 [3, 1024], P(None, 'seq')
Inputs may be any that keep to these rules, and one draw needn't show every extreme that they name: Memory slots 0 to mem_len - 1 of a row are live. With tiles of 128 slots a row has ceil(mem_len / 128) live tiles; the 24 rows together have exactly 96, and in every draw the 3 rows of some index of dp have 3 * 7. Decoder slots 0 to dec_len - 1 of a row are live; every index of dp holds a row with dec_len = 128. `mem_seg`: along a row's slots (tile, then position) never falling, from 0 to the row's pair count minus 1, each of these values on some live slot; slots past mem_len hold the last. `dec_seg`: along a row never falling, with the same pair count as the row's mem_seg, each value on some live slot; slots past dec_len hold the last. Every index of dp holds a row whose dec_seg is 0 throughout and whose dec_len is 128.
All inputs are finite; a program needn't handle non-finite values.
Results may differ from a plain program's by a relative error of at most 0.023.
Values may be sent and summed in bfloat16 or wider, within the bound.
No kernel may reach another device: no remote copies, remote signals or barrier semaphores. Data moves between devices by JAX's collectives and lax.ppermute only.
A program may use at most 320 MiB of HBM per device.

v0:
```python
import jax
import jax.numpy as jnp
from jax import lax
from jax.sharding import PartitionSpec as P

HEADS = 16
HEAD_DIM = 64


EPS = 1e-05
NEG = -1e30


def norm_rows(values, gain, shift):
    centre = values - jnp.mean(values, -1, keepdims=True)
    spread = jnp.mean(centre * centre, -1, keepdims=True)
    return centre * lax.rsqrt(spread + EPS) * gain + shift


def exact_gelu(values):
    return jax.nn.gelu(values, approximate=False)


def project(left, weight):
    return jnp.dot(left, weight, preferred_element_type=jnp.float32)


def weight_grad(left, grad_rows):
    flat_left = left.reshape(-1, left.shape[-1])
    flat_grad = grad_rows.reshape(-1, grad_rows.shape[-1])
    return lax.dot_general(
        flat_left, flat_grad, (((0,), (0,)), ((), ())), preferred_element_type=jnp.float32
    )


def back_product(grad_rows, weight):
    return lax.dot_general(
        grad_rows,
        weight,
        (((grad_rows.ndim - 1,), (1,)), ((), ())),
        preferred_element_type=jnp.float32,
    )


def row_total(grad_rows):
    return jnp.sum(grad_rows.astype(jnp.float32).reshape(-1, grad_rows.shape[-1]), 0)


def split_heads(values):
    return values.reshape(values.shape[0], values.shape[1], HEADS, HEAD_DIM)


def masked_scores(query, key_rows, allowed):
    scores = jnp.einsum(
        "rqhd,rkhd->rhqk",
        split_heads(query),
        split_heads(key_rows),
        preferred_element_type=jnp.float32,
    ) * HEAD_DIM ** (-0.5)
    return jnp.where(allowed[:, None], scores, NEG)


def attend(query, key_rows, value_rows, allowed):
    scores = masked_scores(query, key_rows, allowed)
    top_score = jnp.max(scores, -1, keepdims=True)
    expo = jnp.exp(scores - top_score)
    total_sum = jnp.sum(expo, -1, keepdims=True)
    probs = (expo / total_sum).astype(jnp.bfloat16)
    mixed_h = jnp.einsum(
        "rhqk,rkhd->rqhd", probs, split_heads(value_rows), preferred_element_type=jnp.float32
    )
    return (mixed_h.reshape(query.shape).astype(jnp.bfloat16), top_score + jnp.log(total_sum))


def attend_back(query, key_rows, value_rows, allowed, log_total, grad_mixed):
    scores = masked_scores(query, key_rows, allowed)
    probs = jnp.exp(scores - log_total)
    grad_heads = split_heads(grad_mixed)
    grad_probs = jnp.einsum(
        "rqhd,rkhd->rhqk", grad_heads, split_heads(value_rows), preferred_element_type=jnp.float32
    )
    grad_values = jnp.einsum(
        "rhqk,rqhd->rkhd",
        probs.astype(jnp.bfloat16),
        grad_heads,
        preferred_element_type=jnp.float32,
    )
    centre = jnp.sum(probs * grad_probs, -1, keepdims=True)
    grad_scores = (probs * (grad_probs - centre)).astype(jnp.bfloat16)
    head_scale = HEAD_DIM ** (-0.5)
    grad_query = (
        jnp.einsum(
            "rhqk,rkhd->rqhd",
            grad_scores,
            split_heads(key_rows),
            preferred_element_type=jnp.float32,
        )
        * head_scale
    )
    grad_keys = (
        jnp.einsum(
            "rhqk,rqhd->rkhd", grad_scores, split_heads(query), preferred_element_type=jnp.float32
        )
        * head_scale
    )
    return (
        grad_query.reshape(query.shape),
        grad_keys.reshape(key_rows.shape),
        grad_values.reshape(value_rows.shape),
    )


def to_slots(tile_rows, slot_index, slot_count):
    empty_slots = jnp.zeros((slot_count,) + tile_rows.shape[1:], tile_rows.dtype)
    return empty_slots.at[slot_index].set(tile_rows, mode="drop")


def from_slots(buffer, slot_index, live_flat):
    picked = jnp.take(buffer, jnp.minimum(slot_index, buffer.shape[0] - 1), axis=0)
    return jnp.where(live_flat[:, None, None], picked, jnp.zeros_like(picked))


def per_device(
    dec_in,
    memory,
    proj_w,
    out_w,
    ffn_in,
    ffn_out,
    biases,
    out_bias,
    ffn_bias,
    norm_gain,
    norm_bias,
    mem_len,
    dec_len,
    mem_seg,
    dec_seg,
    cotangent,
):
    group_count = lax.axis_size("dp")
    group_index = lax.axis_index("dp")
    part_index = lax.axis_index("seq")
    row_count, query_count, feature_width = dec_in.shape
    tile_count = memory.shape[1]
    tile_part = memory.shape[2]
    tile_full = mem_seg.shape[2]
    dec_full = dec_seg.shape[1]
    mem_full = tile_count * tile_full
    w_proj, w_out, w_first, w_second = (
        lax.all_gather(proj_w, ("dp", "seq"), axis=1, tiled=True),
        lax.all_gather(out_w, ("dp", "seq"), axis=1, tiled=True),
        lax.all_gather(ffn_in, ("dp", "seq"), axis=0, tiled=True),
        lax.all_gather(ffn_out, ("dp", "seq"), axis=0, tiled=True),
    )
    own_dlen = lax.dynamic_slice_in_dim(dec_len, group_index * row_count, row_count)
    own_mlen = lax.dynamic_slice_in_dim(mem_len, group_index * row_count, row_count)
    query_pos = part_index * query_count + jnp.arange(query_count, dtype=jnp.int32)
    key_pos = jnp.arange(dec_full, dtype=jnp.int32)
    query_live = query_pos[None, :] < own_dlen[:, None]
    key_live = key_pos[None, :] < own_dlen[:, None]
    query_seg = lax.dynamic_slice_in_dim(dec_seg, part_index * query_count, query_count, 1)
    self_mask = (query_seg[:, :, None] == dec_seg[:, None, :]) & (
        key_pos[None, None, :] <= query_pos[None, :, None]
    ) & key_live[:, None, :] | (key_pos[None, None, :] == query_pos[None, :, None])
    mem_ids = mem_seg.reshape(row_count, mem_full)
    mem_live = jnp.arange(mem_full, dtype=jnp.int32)[None, :] < own_mlen[:, None]
    cross_mask = mem_live[:, None, :] & (
        (query_seg[:, :, None] == mem_ids[:, None, :]) | ~query_live[:, :, None]
    )
    tile_counts = (mem_len + tile_full - 1) // tile_full
    tile_firsts = jnp.cumsum(tile_counts) - tile_counts
    group_firsts = tile_firsts.reshape(group_count, row_count)[:, 0]
    own_counts = lax.dynamic_slice_in_dim(tile_counts, group_index * row_count, row_count)
    own_firsts = lax.dynamic_slice_in_dim(tile_firsts, group_index * row_count, row_count)
    capacity = -(-(row_count * tile_count) // group_count)
    slot_count = group_count * capacity
    tile_order = jnp.arange(tile_count, dtype=jnp.int32)
    live_tile = tile_order[None, :] < own_counts[:, None]
    serial = own_firsts[:, None] + tile_order[None, :]
    send_index = jnp.where(
        live_tile,
        serial % group_count * capacity + (serial - own_firsts[0]) // group_count,
        slot_count,
    ).reshape(-1)
    live_flat = live_tile.reshape(-1)
    balanced = (tile_count + 1) // 2 * row_count
    serial_in = jnp.arange(balanced, dtype=jnp.int32) * group_count + group_index
    source = jnp.sum((group_firsts[None, :] <= serial_in[:, None]).astype(jnp.int32), 1) - 1
    source_hit = jnp.arange(group_count, dtype=jnp.int32)[None, :] == source[:, None]
    source_first = jnp.sum(jnp.where(source_hit, group_firsts[None, :], 0), 1)
    recv_index = source * capacity + (serial_in - source_first) // group_count
    query_low = (project(dec_in, w_proj[0]) + biases[0]).astype(jnp.bfloat16)
    key_own = project(dec_in, w_proj[1]).astype(jnp.bfloat16)
    value_own = (project(dec_in, w_proj[2]) + biases[1]).astype(jnp.bfloat16)
    key_all, value_all = (
        lax.all_gather(key_own, "seq", axis=1, tiled=True),
        lax.all_gather(value_own, "seq", axis=1, tiled=True),
    )
    flat_tiles = memory.reshape(row_count * tile_count, tile_part, feature_width)
    arrived = lax.all_to_all(
        to_slots(flat_tiles, send_index, slot_count), "dp", split_axis=0, concat_axis=0, tiled=True
    )
    packed = jnp.take(arrived, recv_index, axis=0)
    packed_keys = project(packed, w_proj[4]).astype(jnp.bfloat16)
    packed_values = (project(packed, w_proj[5]) + biases[3]).astype(jnp.bfloat16)
    home_keys, home_values = (
        lax.all_to_all(
            to_slots(packed_keys, recv_index, slot_count),
            "dp",
            split_axis=0,
            concat_axis=0,
            tiled=True,
        ),
        lax.all_to_all(
            to_slots(packed_values, recv_index, slot_count),
            "dp",
            split_axis=0,
            concat_axis=0,
            tiled=True,
        ),
    )
    tile_shape = (row_count, tile_count, tile_part, feature_width)
    cross_key_own = from_slots(home_keys, send_index, live_flat).reshape(tile_shape)
    cross_value_own = from_slots(home_values, send_index, live_flat).reshape(tile_shape)
    mixed_self, self_lse = attend(query_low, key_all, value_all, self_mask)
    branch_self = project(mixed_self, w_out[0]) + out_bias
    hidden_one, norm_one_back = jax.vjp(
        norm_rows, dec_in.astype(jnp.float32) + branch_self, norm_gain[0], norm_bias[0]
    )
    hidden_one_low = hidden_one.astype(jnp.bfloat16)
    query_two = (project(hidden_one_low, w_proj[3]) + biases[2]).astype(jnp.bfloat16)
    cross_keys, cross_values = (
        lax.all_gather(cross_key_own, "seq", axis=2, tiled=True),
        lax.all_gather(cross_value_own, "seq", axis=2, tiled=True),
    )
    cross_keys = cross_keys.reshape(row_count, mem_full, feature_width)
    cross_values = cross_values.reshape(row_count, mem_full, feature_width)
    mixed_cross, cross_lse = attend(query_two, cross_keys, cross_values, cross_mask)
    branch_cross = project(mixed_cross, w_out[1]) + biases[4]
    hidden_two, norm_two_back = jax.vjp(
        norm_rows, hidden_one + branch_cross, norm_gain[1], norm_bias[1]
    )
    hidden_two_low = hidden_two.astype(jnp.bfloat16)
    inner = project(hidden_two_low, w_first) + ffn_bias
    active, gelu_back = jax.vjp(exact_gelu, inner)
    active_low = active.astype(jnp.bfloat16)
    branch_ffn = project(active_low, w_second) + biases[5]
    normed, norm_three_back = jax.vjp(
        norm_rows, hidden_two + branch_ffn, norm_gain[2], norm_bias[2]
    )
    live_rows = query_live[:, :, None].astype(jnp.float32)
    mixed_out = (normed * live_rows).astype(jnp.bfloat16)
    grad_three, gain_three, shift_three = norm_three_back(cotangent.astype(jnp.float32) * live_rows)
    grad_ffn_low = grad_three.astype(jnp.bfloat16)
    grad_second = weight_grad(active_low, grad_ffn_low)
    bias_ffn_out = row_total(grad_ffn_low)
    (grad_inner,) = gelu_back(back_product(grad_ffn_low, w_second))
    grad_inner_low = grad_inner.astype(jnp.bfloat16)
    grad_first = weight_grad(hidden_two_low, grad_inner_low)
    grad_ffn_bias = row_total(grad_inner_low)
    grad_two, gain_two, shift_two = norm_two_back(
        back_product(grad_inner_low, w_first) + grad_three
    )
    grad_cross_low = grad_two.astype(jnp.bfloat16)
    grad_out_two = weight_grad(mixed_cross, grad_cross_low)
    bias_cross_out = row_total(grad_cross_low)
    grad_mixed_cross = back_product(grad_cross_low, w_out[1]).astype(jnp.bfloat16)
    grad_q2, grad_k2, grad_v2 = attend_back(
        query_two, cross_keys, cross_values, cross_mask, cross_lse, grad_mixed_cross
    )
    full_shape = (row_count, tile_count, tile_full, feature_width)
    summed_k2, summed_v2 = (
        lax.psum_scatter(
            grad_k2.reshape(full_shape).astype(jnp.bfloat16), "seq", scatter_dimension=2, tiled=True
        ).astype(jnp.float32),
        lax.psum_scatter(
            grad_v2.reshape(full_shape).astype(jnp.bfloat16), "seq", scatter_dimension=2, tiled=True
        ).astype(jnp.float32),
    )
    tiles_k2 = summed_k2.astype(jnp.bfloat16).reshape(
        row_count * tile_count, tile_part, feature_width
    )
    tiles_v2 = summed_v2.astype(jnp.bfloat16).reshape(
        row_count * tile_count, tile_part, feature_width
    )
    grad_q2_low = grad_q2.astype(jnp.bfloat16)
    grad_query_two = weight_grad(hidden_one_low, grad_q2_low)
    bias_query_two = row_total(grad_q2_low)
    back_keys, back_values = (
        lax.all_to_all(
            to_slots(tiles_k2, send_index, slot_count),
            "dp",
            split_axis=0,
            concat_axis=0,
            tiled=True,
        ),
        lax.all_to_all(
            to_slots(tiles_v2, send_index, slot_count),
            "dp",
            split_axis=0,
            concat_axis=0,
            tiled=True,
        ),
    )
    packed_gk = jnp.take(back_keys, recv_index, axis=0)
    packed_gv = jnp.take(back_values, recv_index, axis=0)
    grad_key_two = weight_grad(packed, packed_gk)
    grad_value_two = weight_grad(packed, packed_gv)
    bias_value_two = row_total(packed_gv)
    packed_mem = (back_product(packed_gk, w_proj[4]) + back_product(packed_gv, w_proj[5])).astype(
        jnp.bfloat16
    )
    home_mem = lax.all_to_all(
        to_slots(packed_mem, recv_index, slot_count), "dp", split_axis=0, concat_axis=0, tiled=True
    )
    grad_memory = from_slots(home_mem, send_index, live_flat).reshape(tile_shape)
    grad_one, gain_one, shift_one = norm_one_back(back_product(grad_q2_low, w_proj[3]) + grad_two)
    grad_self_low = grad_one.astype(jnp.bfloat16)
    grad_out_one = weight_grad(mixed_self, grad_self_low)
    bias_self_out = row_total(grad_self_low)
    grad_mixed_self = back_product(grad_self_low, w_out[0]).astype(jnp.bfloat16)
    grad_q, grad_k, grad_v = attend_back(
        query_low, key_all, value_all, self_mask, self_lse, grad_mixed_self
    )
    summed_k, summed_v = (
        lax.psum_scatter(
            grad_k.astype(jnp.bfloat16), "seq", scatter_dimension=1, tiled=True
        ).astype(jnp.float32),
        lax.psum_scatter(
            grad_v.astype(jnp.bfloat16), "seq", scatter_dimension=1, tiled=True
        ).astype(jnp.float32),
    )
    grad_q_low = grad_q.astype(jnp.bfloat16)
    grad_k_low = summed_k.astype(jnp.bfloat16)
    grad_v_low = summed_v.astype(jnp.bfloat16)
    grad_tokens = (
        grad_one
        + back_product(grad_q_low, w_proj[0])
        + back_product(grad_k_low, w_proj[1])
        + back_product(grad_v_low, w_proj[2])
    )
    grad_proj = jnp.stack(
        [
            weight_grad(dec_in, grad_q_low),
            weight_grad(dec_in, grad_k_low),
            weight_grad(dec_in, grad_v_low),
            grad_query_two,
            grad_key_two,
            grad_value_two,
        ]
    )
    grad_outs = jnp.stack([grad_out_one, grad_out_two])
    grad_biases = jnp.stack(
        [
            row_total(grad_q_low),
            row_total(grad_v_low),
            bias_query_two,
            bias_value_two,
            bias_cross_out,
            bias_ffn_out,
        ]
    )
    grad_gains = jnp.stack([gain_one, gain_two, gain_three])
    grad_shifts = jnp.stack([shift_one, shift_two, shift_three])
    (
        share_proj,
        share_out,
        share_first,
        share_second,
        share_bias,
        share_out_bias,
        share_ffn_bias,
        share_gain,
        share_shift,
    ) = (
        lax.psum_scatter(
            grad_proj.astype(jnp.bfloat16), "seq", scatter_dimension=1, tiled=True
        ).astype(jnp.float32),
        lax.psum_scatter(
            grad_outs.astype(jnp.bfloat16), "seq", scatter_dimension=1, tiled=True
        ).astype(jnp.float32),
        lax.psum_scatter(
            grad_first.astype(jnp.bfloat16), "seq", scatter_dimension=0, tiled=True
        ).astype(jnp.float32),
        lax.psum_scatter(
            grad_second.astype(jnp.bfloat16), "seq", scatter_dimension=0, tiled=True
        ).astype(jnp.float32),
        lax.psum_scatter(
            grad_biases.astype(jnp.bfloat16), "seq", scatter_dimension=1, tiled=True
        ).astype(jnp.float32),
        lax.psum_scatter(
            bias_self_out.astype(jnp.bfloat16), "seq", scatter_dimension=0, tiled=True
        ).astype(jnp.float32),
        lax.psum_scatter(
            grad_ffn_bias.astype(jnp.bfloat16), "seq", scatter_dimension=0, tiled=True
        ).astype(jnp.float32),
        lax.psum_scatter(
            grad_gains.astype(jnp.bfloat16), "seq", scatter_dimension=1, tiled=True
        ).astype(jnp.float32),
        lax.psum_scatter(
            grad_shifts.astype(jnp.bfloat16), "seq", scatter_dimension=1, tiled=True
        ).astype(jnp.float32),
    )
    totals = lax.psum(
        (
            share_proj,
            share_out,
            share_first,
            share_second,
            share_bias,
            share_out_bias,
            share_ffn_bias,
            share_gain,
            share_shift,
        ),
        "dp",
    )
    return (
        mixed_out,
        grad_tokens,
        grad_memory,
        totals[0],
        totals[1],
        totals[2],
        totals[3],
        totals[4],
        totals[5],
        totals[6],
        totals[7],
        totals[8],
    )


def solution(mesh):
    in_specs = (
        P("dp", "seq", None),
        P("dp", None, "seq", None),
        P(None, ("dp", "seq"), None),
        P(None, ("dp", "seq"), None),
        P(("dp", "seq"), None),
        P(("dp", "seq"), None),
        P(),
        P(),
        P(),
        P(),
        P(),
        P(),
        P(),
        P("dp", None, None),
        P("dp", None),
        P("dp", "seq", None),
    )
    out_specs = (
        P("dp", "seq", None),
        P("dp", "seq", None),
        P("dp", None, "seq", None),
        P(None, "seq", None),
        P(None, "seq", None),
        P("seq", None),
        P("seq", None),
        P(None, "seq"),
        P("seq"),
        P("seq"),
        P(None, "seq"),
        P(None, "seq"),
    )
    return jax.shard_map(
        per_device, mesh=mesh, in_specs=in_specs, out_specs=out_specs, check_vma=False
    )
```

profile of v0, /device:TPU:2, one launch (start us, length us, event | category | flops | bytes accessed | tf_op | source)
XLA Modules:
  0.0 1875.1 jit_solution(3723910732994135340)
XLA Ops:
  12.8 5.5 scatter_fusion
  18.3 4.2 all-to-all-start
  23.0 20.4 %all-to-all-done = bf16[24,32,1024]{2,1,0:T(8,128)(2,1)S(1)} async-done(((bf16[24,32,1024]{2,1,0:T(8,128)(2,1)}), bf16[24,32,1024]{2,1,0:T(8,128)(2,1)S(1)}, u32[]{:S(2)}, u32[]{:S(2)}) %all-to-all-start) | async-done | bytes 1572896 | tf_op jit(solution)/shard_map/all_to_all | solution.py:201
  43.9 69.0 %all-gather.7.cloned.1.call-done = bf16[6,1024,1024]{2,1,0:T(8,128)(2,1)} async-done(((bf16[6,32,1024]{2,1,0:T(8,128)(2,1)}), bf16[6,1024,1024]{2,1,0:T(8,128)(2,1)}) %all-gather.7.cloned.1.call-update) | async-done | bytes 12582928 | tf_op jit(solution)/shard_map/all_gather | solution.py:151
  112.9 2.6 fusion.43
  116.9 2.8 scatter_fusion.2
  119.6 4.2 all-to-all-start.2
  123.9 2.6 add_convert_fusion.2
  127.9 2.8 scatter_fusion.1
  130.7 12.9 all-to-all-done.2
  143.6 5.0 all-to-all-start.1
  150.6 21.4 %all-to-all-done.1 = bf16[24,32,1024]{2,1,0:T(8,128)(2,1)S(1)} async-done(((bf16[24,32,1024]{2,1,0:T(8,128)(2,1)}), bf16[24,32,1024]{2,1,0:T(8,128)(2,1)S(1)}, u32[]{:S(2)}, u32[]{:S(2)}) %all-to-all-start.1) | async-done | bytes 1572896 | tf_op jit(solution)/shard_map/all_to_all | solution.py:215
  173.8 3.2 select_select_fusion.1
  181.8 19.2 %all_gather.25 = bf16[3,128,1024]{2,1,0:T(8,128)(2,1)S(1)} all-gather(bf16[3,32,1024]{2,1,0:T(8,128)(2,1)S(1)} %fusion.72), channel_id=1, replica_groups=mesh['dp'=8,'seq'=4] {'seq'}, dimensions={1}, use_global_device_ids=true | all-gather | bytes 983040 | tf_op jit(solution)/shard_map/all_gather | solution.py:198
  203.7 31.3 %all_gather.26 = bf16[3,128,1024]{2,1,0:T(8,128)(2,1)S(1)} all-gather(bf16[3,32,1024]{2,1,0:T(8,128)(2,1)S(1)} %fusion.77), channel_id=1, replica_groups=mesh['dp'=8,'seq'=4] {'seq'}, dimensions={1}, use_global_device_ids=true | all-gather | bytes 983040 | tf_op jit(solution)/shard_map/all_gather | solution.py:197
  245.2 55.9 %all-gather.11.cloned.1.call-done = bf16[3,7,128,1024]{3,2,1,0:T(8,128)(2,1)} async-done(((bf16[3,7,32,1024]{3,2,1,0:T(8,128)(2,1)}), bf16[3,7,128,1024]{3,2,1,0:T(8,128)(2,1)}) %all-gather.11.cloned.1.call-update) | async-done | bytes 5505040 | tf_op jit(solution)/shard_map/all_gather | solution.py:235
  301.1 8.8 copy.104
  309.9 11.9 reshape_reshape.4
  321.8 82.3 %all-gather.13.cloned.1.call-done = bf16[3,7,128,1024]{3,2,1,0:T(8,128)(2,1)} async-done(((bf16[3,7,32,1024]{3,2,1,0:T(8,128)(2,1)}), bf16[3,7,128,1024]{3,2,1,0:T(8,128)(2,1)}) %all-gather.13.cloned.1.call-update) | async-done | bytes 5505040 | tf_op jit(solution)/shard_map/all_gather | solution.py:234
  404.1 8.7 copy.105
  412.8 11.8 reshape_reshape.5
  424.6 4.1 fusion.131
  436.4 46.1 %all-gather.15.cloned.1.call-done = bf16[1024,4096]{1,0:T(8,128)(2,1)} async-done(((bf16[32,4096]{1,0:T(8,128)(2,1)}), bf16[1024,4096]{1,0:T(8,128)(2,1)}) %all-gather.15.cloned.1.call-update) | async-done | bytes 8388624 | tf_op jit(solution)/shard_map/all_gather | solution.py:153
  482.5 6.5 fusion.87
  489.1 72.2 %all-gather.17.cloned.1.call-done = bf16[4096,1024]{1,0:T(8,128)(2,1)} async-done(((bf16[128,1024]{1,0:T(8,128)(2,1)}), bf16[4096,1024]{1,0:T(8,128)(2,1)}) %all-gather.17.cloned.1.call-update) | async-done | bytes 8388624 | tf_op jit(solution)/shard_map/all_gather | solution.py:154
  561.3 8.7 fusion.133
  572.2 7.2 fusion.136
  579.4 2.9 multiply_reduce_fusion.3
  584.4 6.7 convert_bitcast_fusion
  591.1 11.6 convert_element_type.291
  602.7 9.5 copy.120
  612.4 6.0 multiply_reduce_fusion
  624.0 2.8 multiply_reduce_fusion.4
  632.2 5.8 fusion.8
  638.0 11.6 convert_element_type.287
  649.6 9.6 copy.117
  669.6 4.0 pad_maximum_fusion
  673.6 48.2 %reduce-scatter.22.cloned.1.call-done = bf16[3,7,32,1024]{3,1,0,2:T(8,128)(2,1)} async-done(((bf16[3,7,128,1024]{3,1,0,2:T(8,128)(2,1)}), bf16[3,7,32,1024]{3,1,0,2:T(8,128)(2,1)}) %reduce-scatter.22.cloned.1.call-update) | async-done | bytes 1376272 | tf_op jit(solution)/shard_map/reduce_scatter | solution.py:277
  725.4 5.5 scatter_fusion.4
  730.9 4.2 all-to-all-start.4
  738.9 9.1 reduce-scatter.18.cloned.1.call-done
  749.6 5.0 all-to-all-done.4
  757.7 6.4 bitcast_convert_fusion.1
  765.6 7.7 bitcast_convert_fusion
  773.3 87.0 %reduce-scatter.20.cloned.1.call-done = bf16[3,7,32,1024]{3,1,0,2:T(8,128)(2,1)} async-done(((bf16[3,7,128,1024]{3,1,0,2:T(8,128)(2,1)}), bf16[3,7,32,1024]{3,1,0,2:T(8,128)(2,1)}) %reduce-scatter.20.cloned.1.call-update) | async-done | bytes 1376272 | tf_op jit(solution)/shard_map/reduce_scatter | solution.py:274
  863.9 5.5 scatter_fusion.3
  869.4 4.3 all-to-all-start.3
  876.4 10.5 reduce-scatter.16.cloned.1.call-done
  886.9 3.0 bitcast_dynamic-update-slice_fusion.1
  895.7 4.2 bitcast_dynamic-update-slice_fusion.4
  899.9 2.8 bitcast_dynamic-update-slice_fusion.3
  902.7 2.7 fusion.25
  905.4 2.6 add_convert_fusion
  909.4 2.8 scatter_fusion.5
  912.2 4.3 all-to-all-start.5
  918.4 18.1 all-reduce.3
  943.3 3.1 fusion.59
  946.5 59.6 %reduce-scatter.26.cloned.1.call-done = bf16[2,256,1024]{2,1,0:T(8,128)(2,1)} async-done(((bf16[2,1024,1024]{2,1,0:T(8,128)(2,1)}), bf16[2,256,1024]{2,1,0:T(8,128)(2,1)}) %reduce-scatter.26.cloned.1.call-update) | async-done | bytes 1048592 | tf_op jit(solution)/shard_map/reduce_scatter | solution.py:380
  1006.1 21.6 %reduce-scatter.32.cloned.1.call-done = bf16[6,256]{1,0:T(8,128)(2,1)} async-done(((bf16[6,1024]{1,0:T(8,128)(2,1)}), bf16[6,256]{1,0:T(8,128)(2,1)}) %reduce-scatter.32.cloned.1.call-update) | async-done | bytes 3088 | tf_op jit(solution)/shard_map/reduce_scatter | solution.py:389
  1029.8 142.7 %reduce-scatter.28.cloned.1.call-done = bf16[256,4096]{1,0:T(8,128)(2,1)} async-done(((bf16[1024,4096]{1,0:T(8,128)(2,1)}), bf16[256,4096]{1,0:T(8,128)(2,1)}) %reduce-scatter.28.cloned.1.call-update) | async-done | bytes 2097168 | tf_op jit(solution)/shard_map/reduce_scatter | solution.py:383
  1172.6 147.4 %reduce-scatter.30.cloned.1.call-done = bf16[1024,1024]{1,0:T(8,128)(2,1)} async-done(((bf16[4096,1024]{1,0:T(8,128)(2,1)}), bf16[1024,1024]{1,0:T(8,128)(2,1)}) %reduce-scatter.30.cloned.1.call-update) | async-done | bytes 2097168 | tf_op jit(solution)/shard_map/reduce_scatter | solution.py:386
  1320.0 214.8 %reduce-scatter.24.cloned.1.call-done = bf16[6,256,1024]{1,2,0:T(8,128)(2,1)} async-done(((bf16[6,1024,1024]{1,2,0:T(8,128)(2,1)}), bf16[6,256,1024]{1,2,0:T(8,128)(2,1)}) %reduce-scatter.24.cloned.1.call-update) | async-done | bytes 3145744 | tf_op jit(solution)/shard_map/reduce_scatter | solution.py:377
  1534.8 326.8 %all-reduce.5 = (f32[6,256,1024]{1,2,0:T(8,128)}, f32[2,256,1024]{2,1,0:T(8,128)}, f32[256,4096]{1,0:T(8,128)}, f32[1024,1024]{1,0:T(8,128)}, f32[6,256]{1,0:T(8...) all-reduce(bf16[6,256,1024]{1,2,0:T(8,128)(2,1)} %reduce-scatter.24, ...), channel_id=1, replica_groups=mesh['dp'=8,'seq'=4] {'dp'}, use_global_device_ids=true, to_apply=%region_32.35 | all-reduce | flops 4198656 | bytes 25194496 | tf_op jit(solution)/shard_map/psum | solution.py:405
  1861.6 6.6 copy.125
  (376 shorter events, 100.1 us)
Async XLA Ops:
  7.2 105.7 %all-gather.7.cloned.1.call-start = ((), (), s32[]{:S(2)}) async-start(), calls=%async_computation.17 | async-start | bytes 12976128 | tf_op jit(solution)/shard_map/all_gather | solution.py:151
  7.9 231.9 %all-gather.9.cloned.1.call-start = ((), (), s32[]{:S(2)}) async-start(), calls=%async_computation.18 | async-start | bytes 4325376 | tf_op jit(solution)/shard_map/all_gather | solution.py:152
  11.5 713.9 %copy-start.51 = (s32[21]{0:T(128)}, s32[21]{0:T(128)S(1)}, u32[]{:S(2)}) copy-start(s32[21]{0:T(128)S(1)} %fusion.112) | copy-start | bytes 256
  18.3 25.0 %all-to-all-start = ((bf16[24,32,1024]{2,1,0:T(8,128)(2,1)}), bf16[24,32,1024]{2,1,0:T(8,128)(2,1)S(1)}, u32[]{:S(2)}, u32[]{:S(2)}) async-start(bf16[24,32,1024]{2,1,0:T(8,128)(2,1)} %scatter_fusion), calls=%async_computation | async-start | bytes 3145728 | tf_op jit(solution)/shard_map/all_to_all | solution.py:201
  22.9 101.0 %copy-start.67 = (pred[12]{0:T(512)(128)(4,1)}, pred[12]{0:T(512)(128)(4,1)S(1)}, u32[]{:S(2)}) copy-start(pred[12]{0:T(512)(128)(4,1)S(1)} %get-tuple-element.98) | copy-start | bytes 40
  22.9 92.6 %copy-start.59 = (s32[1024]{0:T(1024)}, s32[1024]{0:T(1024)S(1)}, u32[]{:S(2)}) copy-start(s32[1024]{0:T(1024)S(1)} %pad_clamp_fusion.1) | copy-start | bytes 12292
  23.0 104.9 %copy-start.49 = (s32[12]{0:T(128)}, s32[12]{0:T(128)S(1)}, u32[]{:S(2)}) copy-start(s32[12]{0:T(128)S(1)} %fusion.111) | copy-start | bytes 148
  43.9 80.0 %copy-start.23 = (bf16[12,32,1024]{2,1,0:T(8,128)(2,1)}, bf16[12,32,1024]{2,1,0:T(8,128)(2,1)S(1)}, u32[]{:S(2)}) copy-start(bf16[12,32,1024]{2,1,0:T(8,128)(2,1)S(1)} %gather_fusion) | copy-start | bytes 2359300
  119.6 23.9 %all-to-all-start.2 = ((bf16[24,32,1024]{2,1,0:T(8,128)(2,1)}), bf16[24,32,1024]{2,1,0:T(8,128)(2,1)S(1)}, u32[]{:S(2)}, u32[]{:S(2)}) async-start(bf16[24,32,1024]{2,1,0:T(8,128)(2,1)} %scatter_fusion.2), calls=%async_computation.2 | async-start | bytes 3145728 | tf_op jit(solution)/shard_map/all_to_all | solution.py:208
  143.6 28.4 %all-to-all-start.1 = ((bf16[24,32,1024]{2,1,0:T(8,128)(2,1)}), bf16[24,32,1024]{2,1,0:T(8,128)(2,1)S(1)}, u32[]{:S(2)}, u32[]{:S(2)}) async-start(bf16[24,32,1024]{2,1,0:T(8,128)(2,1)} %scatter_fusion.1), calls=%async_computation.1 | async-start | bytes 3145728 | tf_op jit(solution)/shard_map/all_to_all | solution.py:215
  148.5 152.5 %all-gather.11.cloned.1.call-start = ((), (), s32[]{:S(2)}) async-start(), calls=%async_computation.19 | async-start | bytes 6881280 | tf_op jit(solution)/shard_map/all_gather | solution.py:235
  148.6 25.1 %copy-start.60 = (pred[21]{0:T(512)(128)(4,1)}, pred[21]{0:T(512)(128)(4,1)S(1)}, u32[]{:S(2)}) copy-start(pred[21]{0:T(512)(128)(4,1)S(1)} %lt.142) | copy-start | bytes 67
  148.8 25.0 %copy-start.62 = (pred[21]{0:T(512)(128)(4,1)}, pred[21]{0:T(512)(128)(4,1)S(1)}, u32[]{:S(2)}) copy-start(pred[21]{0:T(512)(128)(4,1)S(1)} %get-tuple-element.96) | copy-start | bytes 67
  148.8 25.0 %copy-start.58 = (s32[1024]{0:T(1024)}, s32[1024]{0:T(1024)S(1)}, u32[]{:S(2)}) copy-start(s32[1024]{0:T(1024)S(1)} %pad_clamp_fusion) | copy-start | bytes 12292
  150.6 23.2 %copy-start.2 = (bf16[21,32,1024]{2,1,0:T(8,128)(2,1)S(1)}, bf16[21,32,1024]{2,1,0:T(8,128)(2,1)}, u32[]{:S(2)}) copy-start(bf16[21,32,1024]{2,1,0:T(8,128)(2,1)} %gather_fusion.2) | copy-start | bytes 4128772
  177.1 227.0 %all-gather.13.cloned.1.call-start = ((), (), s32[]{:S(2)}) async-start(), calls=%async_computation.20 | async-start | bytes 6881280 | tf_op jit(solution)/shard_map/all_gather | solution.py:234
  177.7 304.8 %all-gather.15.cloned.1.call-start = ((), (), s32[]{:S(2)}) async-start(), calls=%async_computation.21 | async-start | bytes 8650752 | tf_op jit(solution)/shard_map/all_gather | solution.py:153
  178.3 383.1 %all-gather.17.cloned.1.call-start = ((), (), s32[]{:S(2)}) async-start(), calls=%async_computation.22 | async-start | bytes 8650752 | tf_op jit(solution)/shard_map/all_gather | solution.py:154
  178.8 543.0 %reduce-scatter.22.cloned.1.call-start = ((), (), s32[]{:S(2)}) async-start(), calls=%async_computation.26 | async-start | bytes 7864320 | tf_op jit(solution)/shard_map/reduce_scatter | solution.py:277
  179.6 254.2 %copy-start.44 = (f32[1,1024]{1,0:T(1,128)}, f32[1,1024]{1,0:T(1,128)S(1)}, u32[]{:S(2)}) copy-start(f32[1,1024]{1,0:T(1,128)S(1)} %get-tuple-element.111) | copy-start | bytes 12292
  179.6 381.7 %copy-start.66 = (f32[1,1024]{1,0:T(1,128)}, f32[1,1024]{1,0:T(1,128)S(1)}, u32[]{:S(2)}) copy-start(f32[1,1024]{1,0:T(1,128)S(1)} %get-tuple-element.112) | copy-start | bytes 12292
  201.4 37.3 %copy-start.14 = (bf16[3,128,1024]{1,2,0:T(8,128)(2,1)}, bf16[3,128,1024]{1,2,0:T(8,128)(2,1)S(1)}, u32[]{:S(2)}) copy-start(bf16[3,128,1024]{1,2,0:T(8,128)(2,1)S(1)} %copy.99) | copy-start | bytes 2359300
  242.2 384.6 %copy-start.39 = (f32[3,32]{1,0:T(4,128)}, f32[3,32]{1,0:T(4,128)S(1)}, u32[]{:S(2)}) copy-start(f32[3,32]{1,0:T(4,128)S(1)} %fusion.100) | copy-start | bytes 1156
  412.8 18.3 slice-start.2
  424.6 6.4 slice-start.3
  433.8 48.7 %copy-start.73 = (f32[4096]{0:T(1024)S(1)}, f32[4096]{0:T(1024)}, u32[]{:S(2)}) copy-start(f32[4096]{0:T(1024)} %param.28) | copy-start | bytes 49156
  436.2 146.1 %copy-start.11 = (f32[3,32,1024]{2,1,0:T(8,128)}, f32[3,32,1024]{2,1,0:T(8,128)S(1)}, u32[]{:S(2)}) copy-start(f32[3,32,1024]{2,1,0:T(8,128)S(1)} %get-tuple-element.128) | copy-start | bytes 1179652
  436.4 145.9 %copy-start.43 = (f32[3,32]{1,0:T(4,128)}, f32[3,32]{1,0:T(4,128)S(1)}, u32[]{:S(2)}) copy-start(f32[3,32]{1,0:T(4,128)S(1)} %fusion.101) | copy-start | bytes 1156
  489.1 83.1 %copy-start.80 = (u8[32,4096]{1,0:T(8,128)(4,1)}, u8[32,4096]{1,0:T(8,128)(4,1)S(1)}, u32[]{:S(2)}) copy-start(u8[32,4096]{1,0:T(8,128)(4,1)S(1)} %get-tuple-element.62) | copy-start | bytes 393220
  489.1 83.1 %copy-start.82 = (u8[32,4096]{1,0:T(8,128)(4,1)}, u8[32,4096]{1,0:T(8,128)(4,1)S(1)}, u32[]{:S(2)}) copy-start(u8[32,4096]{1,0:T(8,128)(4,1)S(1)} %get-tuple-element.63) | copy-start | bytes 393220
  561.3 10.8 slice-start.8
  561.3 8.7 copy-start.13
  561.3 10.8 slice-start.9
  570.4 9.0 slice-start.6
  572.2 7.2 copy-start.29
  572.2 7.2 slice-start.7
  584.4 6.7 copy-start.3
  612.2 8.8 slice-start.4
  612.3 135.7 %reduce-scatter.18.cloned.1.call-start = ((), (), s32[]{:S(2)}) async-start(), calls=%async_computation.24 | async-start | bytes 983040 | tf_op jit(solution)/shard_map/reduce_scatter | solution.py:330
  612.3 6.6 slice-start
  612.3 7.3 slice-start.1
  612.4 8.7 slice-start.5
  632.2 228.1 %reduce-scatter.20.cloned.1.call-start = ((), (), s32[]{:S(2)}) async-start(), calls=%async_computation.25 | async-start | bytes 7864320 | tf_op jit(solution)/shard_map/reduce_scatter | solution.py:274
  659.2 227.7 %reduce-scatter.16.cloned.1.call-start = ((), (), s32[]{:S(2)}) async-start(), calls=%async_computation.23 | async-start | bytes 983040 | tf_op jit(solution)/shard_map/reduce_scatter | solution.py:327
  663.5 275.6 %reduce-scatter.34.cloned.1.call-start = ((), (), s32[]{:S(2)}) async-start(), calls=%async_computation.32 | async-start | bytes 327680
  668.3 271.7 %reduce-scatter.36.cloned.1.call-start = ((), (), s32[]{:S(2)}) async-start(), calls=%async_computation.33 | async-start | bytes 327680
  669.3 336.8 %reduce-scatter.26.cloned.1.call-start = ((), (), s32[]{:S(2)}) async-start(), calls=%async_computation.28 | async-start | bytes 5242880 | tf_op jit(solution)/shard_map/reduce_scatter | solution.py:380
  730.9 23.7 %all-to-all-start.4 = ((bf16[24,32,1024]{2,1,0:T(8,128)(2,1)}), bf16[24,32,1024]{2,1,0:T(8,128)(2,1)S(1)}, u32[]{:S(2)}, u32[]{:S(2)}) async-start(bf16[24,32,1024]{2,1,0:T(8,128)(2,1)} %scatter_fusion.4), calls=%async_computation.8 | async-start | bytes 3145728 | tf_op jit(solution)/shard_map/all_to_all | solution.py:298
  735.0 292.7 %reduce-scatter.32.cloned.1.call-start = ((), (), s32[]{:S(2)}) async-start(), calls=%async_computation.31 | async-start | bytes 20480 | tf_op jit(solution)/shard_map/reduce_scatter | solution.py:389
  736.4 21.3 %copy-start.12 = (f32[3,32,1024]{2,1,0:T(8,128)S(1)}, f32[3,32,1024]{2,1,0:T(8,128)}, u32[]{:S(2)}) copy-start(f32[3,32,1024]{2,1,0:T(8,128)} %copy-done.11) | copy-start | bytes 1179652
  736.4 21.3 %copy-start.17 = (bf16[3,32,4096]{2,1,0:T(8,128)(2,1)S(1)}, bf16[3,32,4096]{2,1,0:T(8,128)(2,1)}, u32[]{:S(2)}) copy-start(bf16[3,32,4096]{2,1,0:T(8,128)(2,1)} %copy-done.16) | copy-start | bytes 2359300
  757.6 415.0 %reduce-scatter.28.cloned.1.call-start = ((), (), s32[]{:S(2)}) async-start(), calls=%async_computation.29 | async-start | bytes 10485760 | tf_op jit(solution)/shard_map/reduce_scatter | solution.py:383
  764.1 555.9 %reduce-scatter.30.cloned.1.call-start = ((), (), s32[]{:S(2)}) async-start(), calls=%async_computation.30 | async-start | bytes 10485760 | tf_op jit(solution)/shard_map/reduce_scatter | solution.py:386
  773.3 90.6 %copy-start.52 = (s32[21]{0:T(128)S(1)}, s32[21]{0:T(128)}, u32[]{:S(2)}) copy-start(s32[21]{0:T(128)} %copy-done.51) | copy-start | bytes 256
  869.4 24.7 %all-to-all-start.3 = ((bf16[24,32,1024]{2,1,0:T(8,128)(2,1)}), bf16[24,32,1024]{2,1,0:T(8,128)(2,1)S(1)}, u32[]{:S(2)}, u32[]{:S(2)}) async-start(bf16[24,32,1024]{2,1,0:T(8,128)(2,1)} %scatter_fusion.3), calls=%async_computation.6 | async-start | bytes 3145728 | tf_op jit(solution)/shard_map/all_to_all | solution.py:291
  873.7 661.1 %reduce-scatter.24.cloned.1.call-start = ((), (), s32[]{:S(2)}) async-start(), calls=%async_computation.27 | async-start | bytes 15728640 | tf_op jit(solution)/shard_map/reduce_scatter | solution.py:377
  876.4 13.5 copy-start.22
  912.2 24.4 %copy-start.8 = (f32[3,32,1024]{2,1,0:T(8,128)S(1)}, f32[3,32,1024]{2,1,0:T(8,128)}, u32[]{:S(2)}) copy-start(f32[3,32,1024]{2,1,0:T(8,128)} %copy-done.7) | copy-start | bytes 1179652
  912.2 24.4 %copy-start.42 = (f32[3,32]{1,0:T(4,128)S(1)}, f32[3,32]{1,0:T(4,128)}, u32[]{:S(2)}) copy-start(f32[3,32]{1,0:T(4,128)} %copy-done.41) | copy-start | bytes 1156
  912.2 115.5 %all-to-all-start.5 = ((bf16[24,32,1024]{2,1,0:T(8,128)(2,1)}), bf16[24,32,1024]{2,1,0:T(8,128)(2,1)S(1)}, u32[]{:S(2)}, u32[]{:S(2)}) async-start(bf16[24,32,1024]{2,1,0:T(8,128)(2,1)} %scatter_fusion.5), calls=%async_computation.9 | async-start | bytes 3145728 | tf_op jit(solution)/shard_map/all_to_all | solution.py:314
  946.5 82.0 %copy-start.61 = (pred[21]{0:T(512)(128)(4,1)S(1)}, pred[21]{0:T(512)(128)(4,1)}, u32[]{:S(2)}) copy-start(pred[21]{0:T(512)(128)(4,1)} %copy-done.60) | copy-start | bytes 67
  946.5 82.0 %copy-start.63 = (pred[21]{0:T(512)(128)(4,1)S(1)}, pred[21]{0:T(512)(128)(4,1)}, u32[]{:S(2)}) copy-start(pred[21]{0:T(512)(128)(4,1)} %copy-done.62) | copy-start | bytes 67
  1028.5 506.4 %copy-start.21 = (bf16[2,256,1024]{2,1,0:T(8,128)(2,1)S(1)}, bf16[2,256,1024]{2,1,0:T(8,128)(2,1)}, u32[]{:S(2)}) copy-start(bf16[2,256,1024]{2,1,0:T(8,128)(2,1)} %reduce-scatter.26.cloned.1.call-done) | copy-start | bytes 3145732
  1028.5 506.3 %copy-start.64 = (bf16[6,256]{1,0:T(8,128)(2,1)S(1)}, bf16[6,256]{1,0:T(8,128)(2,1)}, u32[]{:S(2)}) copy-start(bf16[6,256]{1,0:T(8,128)(2,1)} %reduce-scatter.32.cloned.1.call-done) | copy-start | bytes 9220
  (53 other events, 137.5 us)
Sparse Core Ops, SparseCore 0:
  11.0 101.8 all-gather.6
  115.9 68.9 all-gather.8
  187.1 113.9 all-gather.10
  303.1 100.9 all-gather.12
  406.8 75.6 all-gather.14
  485.3 75.9 all-gather.16
  612.4 109.3 reduce-scatter.21
  724.1 23.8 reduce-scatter.17
  750.3 109.9 reduce-scatter.19
  863.0 23.8 reduce-scatter.15
  889.2 18.8 reduce-scatter.33
  910.3 17.8 reduce-scatter.35
  931.1 74.9 reduce-scatter.25
  1008.3 19.3 reduce-scatter.31
  1029.9 142.6 reduce-scatter.27
  1174.8 145.1 reduce-scatter.29
  1322.2 212.5 reduce-scatter.23
where the time goes:
time: 1890 us; the launch traced here: 1880 us
  waiting for transfers between devices  1130 us (60%)
  blocking collectives  395 us (21%)
  local copies, waits for them, and re-layouts  158 us (8%)
  matrix products  126 us (7%)
  starting transfers between devices  27.2 us (1%)
  other arithmetic  22 us (1%)
    psum x1, blocking collectives, per_device(): lax.psum((share_proj, share_out, share_first, share_second, share_bias, s...  327 us
    reduce_scatter x1, waiting for transfers between devices, per_device(): lax.psum_scatter(grad_proj.astype(jnp.bfloat16), 'seq', scatter_dimension...  215 us
    reduce_scatter x1, waiting for transfers between devices, per_device(): lax.psum_scatter(grad_second.astype(jnp.bfloat16), 'seq', scatter_dimensi...  147 us
    reduce_scatter x1, waiting for transfers between devices, per_device(): lax.psum_scatter(grad_first.astype(jnp.bfloat16), 'seq', scatter_dimensio...  143 us
    reduce_scatter x1, waiting for transfers between devices, per_device(): lax.psum_scatter(grad_k2.reshape(full_shape).astype(jnp.bfloat16), 'seq',...  87 us
    all_gather x1, waiting for transfers between devices, per_device(): lax.all_gather(cross_key_own, 'seq', axis=2, tiled=True)  82.3 us
    all_gather x1, waiting for transfers between devices, per_device(): lax.all_gather(ffn_out, ('dp', 'seq'), axis=0, tiled=True)  72.2 us
    all_gather x1, waiting for transfers between devices, per_device(): lax.all_gather(proj_w, ('dp', 'seq'), axis=1, tiled=True)  69 us
  transfers between devices with their start and end apart: 23, of which 18 were waited for; matrix products, arithmetic and copies ran while one was open for 13% of the time, Pallas kernels for 0%

commit v1 on v0

v1 whole, which is shorter than its diff:
```python
import functools

import jax
import jax.numpy as jnp
from jax import lax
from jax.experimental import pallas as pl
from jax.experimental.pallas import tpu as pltpu
from jax.sharding import Mesh
from jax.sharding import PartitionSpec as P

HEADS = 16
HEAD_DIM = 64
LOCAL_HEADS = 4
EPS = 1e-05
NEG = -1e30
F32 = jnp.float32
BF16 = jnp.bfloat16
AXES = ("hi", "x", "core", "z")
ORDER = (0, 2, 1, 3)
VMEM_LIMIT = 60 * 1024 * 1024


def mm(left, right):
    return jnp.dot(left, right, preferred_element_type=F32)


def mm_t(left, right):
    return lax.dot_general(left, right, (((1,), (1,)), ((), ())), preferred_element_type=F32)


def t_mm(left, right):
    return lax.dot_general(left, right, (((0,), (0,)), ((), ())), preferred_element_type=F32)


def pick(array, index, axis=0):
    return lax.dynamic_index_in_dim(array, index, axis, False)


def swap(values, axis):
    return lax.ppermute(values, axis, [(0, 1), (1, 0)])


def head_masks(width):
    lane = lax.broadcasted_iota(jnp.int32, (1, width), 1)
    return [(lane // HEAD_DIM) == h for h in range(LOCAL_HEADS)]


def stack_heads(values, masks):
    zero = jnp.zeros_like(values)
    return jnp.concatenate([jnp.where(m, values, zero) for m in masks], 0)


def join_heads(stacked, masks, rows):
    out = jnp.zeros((rows, stacked.shape[1]), stacked.dtype)
    for h, m in enumerate(masks):
        out = jnp.where(m, stacked[h * rows : (h + 1) * rows], out)
    return out


def softmax_parts(scores, allowed):
    scores = jnp.where(allowed, scores * HEAD_DIM**-0.5, NEG)
    top = jnp.max(scores, -1, keepdims=True)
    expo = jnp.exp(scores - top)
    return expo * (1.0 / jnp.sum(expo, -1, keepdims=True))


def attend_core(q, k, v, allowed):
    rows, width = q.shape
    masks = head_masks(width)
    scores = mm_t(stack_heads(q, masks), k)
    probs = [
        softmax_parts(scores[h * rows : (h + 1) * rows], allowed).astype(BF16)
        for h in range(LOCAL_HEADS)
    ]
    mixed = mm(jnp.concatenate(probs, 0), v)
    return join_heads(mixed, masks, rows).astype(BF16)


def attend_back_core(q, k, v, allowed, grad):
    rows, width = q.shape
    masks = head_masks(width)
    q_heads = stack_heads(q, masks)
    grad_heads = stack_heads(grad, masks)
    scores = mm_t(q_heads, k)
    grad_probs = mm_t(grad_heads, v)
    probs, grad_scores = [], []
    for h in range(LOCAL_HEADS):
        part = slice(h * rows, (h + 1) * rows)
        p = softmax_parts(scores[part], allowed)
        gp = grad_probs[part]
        centre = jnp.sum(p * gp, -1, keepdims=True)
        grad_scores.append((p * (gp - centre)).astype(BF16))
        probs.append(p.astype(BF16))
    probs = jnp.concatenate(probs, 0)
    grad_scores = jnp.concatenate(grad_scores, 0)
    scale = HEAD_DIM**-0.5
    dq = join_heads(mm(grad_scores, k), masks, rows) * scale
    dk = t_mm(grad_scores, q_heads) * scale
    dv = t_mm(probs, grad_heads)
    return dq.astype(BF16), dk.astype(BF16), dv.astype(BF16)


def run(kernel, args, outs, scratch=(), aliases=None, any_args=(), any_outs=()):
    single = not isinstance(outs, (list, tuple))
    out_list = [outs] if single else list(outs)
    vmem = pl.BlockSpec(memory_space=pltpu.VMEM)
    anywhere = pl.BlockSpec(memory_space=pl.ANY)
    base = getattr(kernel, "func", kernel)
    result = pl.pallas_call(
        kernel,
        name=base.__name__,
        in_specs=[anywhere if i in any_args else vmem for i in range(len(args))],
        out_specs=[anywhere if i in any_outs else vmem for i in range(len(out_list))],
        out_shape=out_list,
        scratch_shapes=list(scratch),
        input_output_aliases=aliases or {},
        compiler_params=pltpu.CompilerParams(vmem_limit_bytes=VMEM_LIMIT),
    )(*args)
    return result[0] if single else result


def shaped(shape, dtype):
    return jax.ShapeDtypeStruct(shape, dtype)


def group_place():
    return lax.axis_index("x") * 2 + lax.axis_index("core")


def lanes(start, size):
    return pl.ds(pl.multiple_of(start, 128), size)


def local_bias(ref, row, j):
    n = ref.shape[1]
    return jnp.concatenate(
        [ref[pl.ds(row, 1), lanes(h * (n // 2) + j * (n // 8), n // 8)] for h in range(2)], 1
    )


def whole(refs):
    return jnp.concatenate([r[...] for r in refs], 0)


def halves(product, act, sent_ref, kept_ref):
    half = act.shape[0] // 2
    sent_ref[...] = product(act[half:]).astype(BF16)
    kept_ref[...] = product(act[:half])


def flat_row(ref, r):
    block = ref[:, r]
    return block.reshape(block.shape[0] * block.shape[1], block.shape[2])


def self_fwd_kernel(x0, x1, x2, x3, w, wo, biases, mask, qkv_out, o_out, sent, kept):
    j = group_place()
    tokens = whole([x0, x1, x2, x3])
    width = wo.shape[0]
    bq = local_bias(biases, 0, j)
    bias = jnp.concatenate([bq, jnp.zeros_like(bq), local_bias(biases, 1, j)], 1)
    qkv = (mm(tokens, w[...]) + bias).astype(BF16)
    qkv_out[...] = qkv.reshape(qkv_out.shape)
    for r in range(qkv_out.shape[1]):
        row = flat_row(qkv_out, r)
        out = attend_core(
            row[:, :width], row[:, width : 2 * width], row[:, 2 * width :], mask[r] > 0.5
        )
        o_out[:, r] = out.reshape(o_out.shape[0], o_out.shape[2], width)
    mixed = o_out[...].reshape(tokens.shape[0], width)
    halves(lambda a: mm(a, wo[...]), mixed, sent, kept)


def cross_allowed(qc, kc):
    return (kc >= 0.0) & ((kc == qc) | (qc < -1.5))


def kv_row(kv_refs, r):
    return jnp.concatenate([ref[r] for ref in kv_refs], 0)


def cross_fwd_kernel(
    h0, h1, h2, h3, w, wo, biases, kv0, kv1, kv2, kv3, q_code, k_code, q_out, o_out, sent, kept
):
    j = group_place()
    tokens = whole([h0, h1, h2, h3])
    width = wo.shape[0]
    query = (mm(tokens, w[:, :width]) + local_bias(biases, 2, j)).astype(BF16)
    q_out[...] = query.reshape(q_out.shape)

    def one_row(r, carry):
        kv = kv_row([kv0, kv1, kv2, kv3], r)
        allowed = cross_allowed(q_code[r], k_code[r])
        out = attend_core(flat_row(q_out, r), kv[:, :width], kv[:, width:], allowed)
        o_out[:, r] = out.reshape(o_out.shape[0], o_out.shape[2], width)
        return carry

    lax.fori_loop(0, q_out.shape[1], one_row, 0)
    mixed = o_out[...].reshape(tokens.shape[0], width)
    halves(lambda a: mm(a, wo[...]), mixed, sent, kept)


def ffn_fwd_kernel(h0, h1, h2, h3, w1, w2, bias, g_out, slope_out, sent, kept):
    j = group_place()
    tokens = whole([h0, h1, h2, h3])
    u = mm(tokens, w1[...]) + local_bias(bias, 0, j)
    normal = 0.5 * (1.0 + lax.erf(u * 0.7071067811865476))
    slope_out[...] = normal + u * (0.3989422804014327 * jnp.exp(-0.5 * u * u))
    g_out[...] = (u * normal).astype(BF16)
    halves(lambda a: mm(a, w2[...]), g_out[...], sent, kept)


def ffn_bwd_kernel(f0, f1, f2, f3, w1, w2, slope, du_out, bias_out, sent, kept):
    grads = whole([f0, f1, f2, f3])
    du = (mm_t(grads, w2[...]) * slope[...]).astype(BF16)
    du_out[...] = du
    bias_out[...] = jnp.sum(du.astype(F32), 0, keepdims=True)
    halves(lambda a: mm_t(a, w1[...]), du, sent, kept)


def cross_bwd_kernel(
    f0, f1, f2, f3, w, wo, q, kv0, kv1, kv2, kv3, q_code, k_code,
    dq_out, dkv0, dkv1, dkv2, dkv3, sums, sent, kept, do_ref,
):
    grads = whole([f0, f1, f2, f3])
    width = wo.shape[0]
    do_ref[...] = mm_t(grads, wo[...]).astype(BF16).reshape(do_ref.shape)
    slots = kv0.shape[1]
    sums[...] = jnp.zeros_like(sums)

    def one_row(r, carry):
        kv = kv_row([kv0, kv1, kv2, kv3], r)
        allowed = cross_allowed(q_code[r], k_code[r])
        dq, dk, dv = attend_back_core(
            flat_row(q, r), kv[:, :width], kv[:, width:], allowed, flat_row(do_ref, r)
        )
        dq_out[:, r] = dq.reshape(dq_out.shape[0], dq_out.shape[2], width)
        dkv = jnp.concatenate([dk, dv], 1)
        for d, ref in enumerate([dkv0, dkv1, dkv2, dkv3]):
            ref[r] = dkv[d * slots : (d + 1) * slots]
        sums[1:2, :] += jnp.sum(dv.astype(F32), 0, keepdims=True)
        return carry

    lax.fori_loop(0, q.shape[1], one_row, 0)
    dq = dq_out[...].reshape(grads.shape[0], width)
    sums[0:1, :] = jnp.sum(dq.astype(F32), 0, keepdims=True)
    halves(lambda a: mm_t(a, w[:, :width]), dq, sent, kept)


def self_bwd_kernel(f0, f1, f2, f3, w, wo, qkv, mask, dqkv_out, sums, sent, kept):
    grads = whole([f0, f1, f2, f3])
    width = wo.shape[0]
    shape = (qkv.shape[0], qkv.shape[1], qkv.shape[2], width)
    do = mm_t(grads, wo[...]).astype(BF16).reshape(shape)
    for r in range(shape[1]):
        row = flat_row(qkv, r)
        grad = do[:, r].reshape(row.shape[0], width)
        parts = attend_back_core(
            row[:, :width], row[:, width : 2 * width], row[:, 2 * width :], mask[r] > 0.5, grad
        )
        dqkv_out[:, r] = jnp.concatenate(parts, 1).reshape(shape[0], shape[2], 3 * width)
    dqkv = dqkv_out[...].reshape(grads.shape[0], 3 * width)
    sums[...] = jnp.sum(dqkv.astype(F32), 0, keepdims=True)
    halves(lambda a: mm_t(a, w[...]), dqkv, sent, kept)


def branch_sum(kept, arrived, crossed):
    n = crossed.shape[0]
    return kept[:n] + arrived[:n].astype(F32) + crossed[...].astype(F32)


def normalise(v):
    centre = v - jnp.mean(v, -1, keepdims=True)
    rstd = lax.rsqrt(jnp.mean(centre * centre, -1, keepdims=True) + EPS)
    return centre * rstd, rstd


def denormalise(e, gain, n, rstd):
    a = e * gain
    return rstd * (a - jnp.mean(a, -1, keepdims=True) - n * jnp.mean(a * n, -1, keepdims=True))


def norm_one_kernel(kept, arrived, crossed, own, bias, gains, shifts, n_out, rstd_out, low_out):
    v = branch_sum(kept, arrived, crossed) + bias[...] + own[...].astype(F32)
    n, rstd = normalise(v)
    n_out[...] = n
    rstd_out[...] = jnp.broadcast_to(rstd, rstd_out.shape)
    low_out[...] = (n * gains[0:1] + shifts[0:1]).astype(BF16)


def norm_two_kernel(kept, arrived, crossed, n_one, biases, gains, shifts, n_out, rstd_out, low_out):
    resid = n_one[...] * gains[0:1] + shifts[0:1]
    n, rstd = normalise(branch_sum(kept, arrived, crossed) + biases[4:5] + resid)
    n_out[...] = n
    rstd_out[...] = jnp.broadcast_to(rstd, rstd_out.shape)
    low_out[...] = (n * gains[1:2] + shifts[1:2]).astype(BF16)


def sums_of(e, n, low):
    return jnp.concatenate(
        [
            jnp.sum(e * n, 0, keepdims=True),
            jnp.sum(e, 0, keepdims=True),
            jnp.sum(low.astype(F32), 0, keepdims=True),
            jnp.zeros((5, e.shape[1]), F32),
        ],
        0,
    )


def norm_three_kernel(
    kept, arrived, crossed, n_two, biases, gains, shifts, cot, live, mixed_out, d_out, low_out, sums
):
    resid = n_two[...] * gains[1:2] + shifts[1:2]
    n, rstd = normalise(branch_sum(kept, arrived, crossed) + biases[5:6] + resid)
    mixed_out[...] = ((n * gains[2:3] + shifts[2:3]) * live[...]).astype(BF16)
    e = cot[...].astype(F32) * live[...]
    d = denormalise(e, gains[2:3], n, rstd)
    low = d.astype(BF16)
    d_out[...] = d
    low_out[...] = low
    sums[...] = sums_of(e, n, low)


def norm_back_kernel(which, kept, arrived, crossed, d_in, n, rstd, gains, d_out, low_out, sums):
    e = branch_sum(kept, arrived, crossed) + d_in[...]
    d = denormalise(e, gains[which : which + 1], n[...], rstd[:, 0:1])
    low = d.astype(BF16)
    d_out[...] = d
    low_out[...] = low
    sums[...] = sums_of(e, n[...], low)


def cut_cols_kernel(proj, first, *outs):
    j = group_place()
    n, _, width = proj.shape
    ff = first.shape[1]
    for d, out in enumerate(outs):
        target = jnp.bitwise_xor(j, d)
        at = 0
        for m in range(n):
            for h in range(2):
                out[:, at : at + width // 8] = proj[
                    m, :, lanes(h * (width // 2) + target * (width // 8), width // 8)
                ]
                at += width // 8
        for h in range(2):
            out[:, at : at + ff // 8] = first[:, lanes(h * (ff // 2) + target * (ff // 8), ff // 8)]
            at += ff // 8


def pack_kernel(e0, e1, e2, e3, out_w, second, buf_a, buf_b, buf_c):
    j = group_place()
    quarter = out_w.shape[2] // 4
    three = 3 * quarter
    rows = e0.shape[0]
    for d, e in enumerate([e0, e1, e2, e3]):
        at = jnp.bitwise_xor(j, d)
        buf_a[at, :, :three] = e[:, :three]
        buf_b[at, :, :three] = e[:, three : 2 * three]
        buf_c[at] = e[:, 2 * three :]
    for i in range(4):
        buf_a[i, :, three:] = out_w[0, :, i * quarter : (i + 1) * quarter]
        buf_b[i, :, three:] = out_w[1, :, i * quarter : (i + 1) * quarter]
        buf_c[4 + i] = second[i * rows : (i + 1) * rows]


def place_kernel(n_z, ffn, *refs):
    blocks, wcol, wrow = refs[: 2 * n_z], refs[2 * n_z], refs[2 * n_z + 1]
    hi = lax.axis_index("hi")
    z = lax.axis_index("z")
    cols = wcol.shape[-1]
    rows = wcol.shape[-2]
    for half in range(2):
        h = hi if half == 0 else 1 - hi
        for k in range(n_z):
            zz = lax.rem(z + k, n_z)
            block = blocks[half * n_z + k]
            for i in range(4):
                if ffn:
                    wcol[h, i, zz] = block[i]
                    wrow[h, zz, i * rows : (i + 1) * rows] = block[4 + i]
                else:
                    wcol[h, i, zz] = block[i, :, :cols]
                    quarter = block.shape[2] - cols
                    wrow[h, zz, :, i * quarter : (i + 1) * quarter] = block[i, :, cols:]


def select_rows(dst, pieces, n_z, half_index):
    z = lax.axis_index("z")
    at = 0
    for piece in pieces:
        count, width = piece.shape
        for k in range(n_z):
            start = lax.rem(z + k, n_z) * (width // n_z) + half_index * (width // n_z // 2)
            dst[at : at + count, k * 128 : (k + 1) * 128] = piece[:, lanes(start, 128)]
        at += count


def select_cols(dst, pieces, n_z):
    z = lax.axis_index("z")
    at = 0
    for piece in pieces:
        count, width = piece.shape
        size = width // n_z
        for k in range(n_z):
            start = lax.rem(z + k, n_z) * size
            dst[at : at + count, k * size : (k + 1) * size] = piece[:, lanes(start, size)]
        at += count


def put_cols(out, at, block):
    n_z, rows = out.shape[0], out.shape[1]
    cols = block.shape[1]
    out[:, :, at : at + cols] = block.astype(BF16).reshape(n_z, rows, cols)


def put_rows(out, at, block):
    n_z, rows = out.shape[0], out.shape[1]
    size = block.shape[1] // n_z
    for k in range(n_z):
        for i in range(block.shape[0] // rows):
            out[k, :, at + i * size : at + (i + 1) * size] = block[
                i * rows : (i + 1) * rows, k * size : (k + 1) * size
            ].astype(BF16)


def half_of(ref, h):
    size = ref.shape[1] // 2
    return ref[:, lanes(h * size, size)]


def ffn_grad_kernel(n_z, a0, a1, a2, a3, du, g, f0, f1, f2, f3, kept, sent, left, right):
    hi = lax.axis_index("hi")
    select_cols(right, [f0, f1, f2, f3], n_z)
    for out, h in ((sent, 1 - hi), (kept, hi)):
        select_rows(left, [a0, a1, a2, a3], n_z, h)
        put_cols(out, 0, t_mm(left[...], du[...]))
        put_rows(out, du.shape[1], t_mm(half_of(g, h), right[...]))


def memory_grad_kernel(n_z, *refs):
    mems, dkvs, kept, sent, left, right, total = refs[:4], refs[4:8], *refs[8:]
    hi = lax.axis_index("hi")
    row = pl.program_id(0)
    slots = mems[0].shape[1]
    for d in range(4):
        right[d * slots : (d + 1) * slots] = dkvs[d][0]
    for s, h in ((0, hi), (1, 1 - hi)):
        select_rows(left, [m.at[0] for m in mems], n_z, h)
        part = t_mm(left[...], right[...])

        @pl.when(row == 0)
        def _():
            total[s] = part

        @pl.when(row > 0)
        def _():
            total[s] += part

    @pl.when(row == pl.num_programs(0) - 1)
    def _():
        put_cols(kept, 0, total[0])
        put_cols(sent, 0, total[1])


def cross_grad_kernel(
    n_z, h0, h1, h2, h3, dq, kv_kept, kv_sent, o2, f20, f21, f22, f23, o1, f10, f11, f12, f13,
    kept, sent, left, right,
):
    hi = lax.axis_index("hi")
    c_q, c_kv = dq.shape[1], kv_kept.shape[2]
    for out, h, kv in ((sent, 1 - hi, kv_sent), (kept, hi, kv_kept)):
        select_rows(left, [h0, h1, h2, h3], n_z, h)
        put_cols(out, 0, t_mm(left[...], dq[...]))
        out[:, :, c_q : c_q + c_kv] = kv[...]
    at = c_q + c_kv
    for o, f in ((o1, [f10, f11, f12, f13]), (o2, [f20, f21, f22, f23])):
        select_cols(right, f, n_z)
        for out, h in ((sent, 1 - hi), (kept, hi)):
            put_rows(out, at, t_mm(half_of(o, h), right[...]))
        at += right.shape[1] // n_z


def self_grad_kernel(n_z, x0, x1, x2, x3, dqkv, sums, kept, sent, left):
    hi = lax.axis_index("hi")
    rows = kept.shape[1] - 16
    cols = dqkv.shape[1]
    lower = jnp.broadcast_to(sums[...], (16, cols)).astype(BF16)
    for out, h in ((sent, 1 - hi), (kept, hi)):
        select_rows(left, [x0, x1, x2, x3], n_z, h)
        block = t_mm(left[...], dqkv[...]).astype(BF16)
        for k in range(n_z):
            out[k, :rows] = block[k * rows : (k + 1) * rows]
            out[k, rows:] = lower


def pair_sum_kernel(kept, arrived, own, *sent):
    own[...] = kept[0].astype(F32) + arrived[0].astype(F32)
    for k, out in enumerate(sent):
        out[...] = (kept[k + 1].astype(F32) + arrived[k + 1].astype(F32)).astype(BF16)


def final_sum_kernel(cols, own, *refs):
    total = own[...]
    arrived, outs = refs[: -len(cols)], refs[-len(cols) :]
    for a in arrived:
        total = total + a[...].astype(F32)
    at = 0
    for out, size in zip(outs, cols):
        out[...] = total[:, at : at + size].astype(BF16)
        at += size


def places(index):
    h = jnp.bitwise_xor(lax.axis_index("hi"), (index >> 2) & 1)
    return h, jnp.bitwise_xor(group_place(), index & 3)


def ffn_out_kernel(*refs):
    pieces, first, second = refs[:8], refs[8], refs[9]
    rows = pieces[0].shape[0]
    ff = first.shape[1]
    width = second.shape[1]
    size = width // 4
    for index, piece in enumerate(pieces):
        h, j = places(index)
        for half in range(2):
            first[
                pl.ds(pl.multiple_of(h * rows, 8), rows),
                lanes(half * (ff // 2) + j * (ff // 8), ff // 8),
            ] = piece[:, half * (ff // 8) : (half + 1) * (ff // 8)].astype(F32)
        for i in range(4):
            at = ff // 4 + i * size
            second[
                pl.ds(pl.multiple_of(h * 4 * rows + i * rows, 8), rows), lanes(j * size, size)
            ] = piece[:, at : at + size].astype(F32)


def place_cols(out, m, rows, piece, at):
    width = out.shape[2]
    for index, p in enumerate(piece):
        h, j = places(index)
        for half in range(2):
            lo = at + half * (width // 8)
            out[
                m,
                pl.ds(pl.multiple_of(h * rows, 8), rows),
                lanes(half * (width // 2) + j * (width // 8), width // 8),
            ] = p[:rows, lo : lo + width // 8].astype(F32)


def cross_out_kernel(*refs):
    pieces, g_proj, g_out, work, sem = refs[:8], *refs[8:]
    rows = pieces[0].shape[0]
    width = work.shape[2]
    for m in range(3):
        place_cols(work, m, rows, pieces, m * (width // 4))
    copy = pltpu.make_async_copy(work, g_proj.at[pl.ds(3, 3)], sem)
    copy.start()
    for index, piece in enumerate(pieces):
        h, j = places(index)
        for m in range(2):
            at = 3 * (width // 4) + m * (width // 4)
            g_out[
                m, pl.ds(pl.multiple_of(h * rows, 8), rows), lanes(j * (width // 4), width // 4)
            ] = piece[:, at : at + width // 4].astype(F32)
    copy.wait()


def self_out_kernel(*refs):
    pieces, _, g_proj, sums, work, sem = refs[:8], *refs[8:]
    rows = pieces[0].shape[0] - 16
    width = work.shape[2]
    for m in range(3):
        place_cols(work, m, rows, pieces, m * (width // 4))
    copy = pltpu.make_async_copy(work, g_proj.at[pl.ds(0, 3)], sem)
    copy.start()
    sums[...] = jnp.zeros_like(sums)
    for index in range(4):
        _, j = places(index)
        for m in range(3):
            for half in range(2):
                lo = m * (width // 4) + half * (width // 8)
                sums[m : m + 1, lanes(half * (width // 2) + j * (width // 8), width // 8)] = (
                    pieces[index][rows : rows + 16, lo : lo + width // 8].astype(F32)[0:1]
                )
    copy.wait()


def small_kernel(s3, s2, s1, cross_sums, ff_sum, out):
    j = group_place()
    width = out.shape[1]
    ff = ff_sum.shape[1] * 4
    out[...] = jnp.zeros_like(out)
    for half in range(2):
        at = lanes(half * (width // 2) + j * (width // 8), width // 8)
        part = slice(half * (width // 8), (half + 1) * (width // 8))
        out[0:1, at] = cross_sums[0:1, part]
        out[1:2, at] = cross_sums[1:2, part]
    out[2:3] = s2[2:3]
    out[3:4] = s3[2:3]
    out[4:5] = s1[2:3]
    ff_rows = ff // width
    per = ff // 8
    for half in range(2):
        flat_at = half * (ff // 2) + j * per
        row = 5 + flat_at // width
        out[pl.ds(row, 1), lanes(lax.rem(flat_at, width), per)] = ff_sum[
            0:1, half * per : (half + 1) * per
        ]
    at = 5 + ff_rows
    for i, s in enumerate([s1, s2, s3]):
        out[at + i : at + i + 1] = s[0:1]
        out[at + 3 + i : at + 4 + i] = s[1:2]


def per_device(
    dec_in,
    memory,
    proj_w,
    out_w,
    ffn_in,
    ffn_out,
    biases,
    out_bias,
    ffn_bias,
    norm_gain,
    norm_bias,
    mem_len,
    dec_len,
    mem_seg,
    dec_seg,
    cotangent,
):
    n_hi = lax.axis_size("hi")
    n_z = lax.axis_size("z")
    hi = lax.axis_index("hi")
    zi = lax.axis_index("z")
    j = group_place()
    fast = n_hi == 2 and n_z == 4
    row_count, query_count, width = dec_in.shape
    tile_count, tile_part = memory.shape[1], memory.shape[2]
    own_tokens = row_count * query_count
    all_tokens = 4 * own_tokens
    slots = tile_count * tile_part
    ff_width = ffn_in.shape[1]
    local = width // 4
    ff_local = ff_width // 4

    def turned(index):
        return (index & 1) * 2 + (index >> 1)

    to_rows = [
        ((h * 4 + a) * 4 + b, (h * 4 + turned(b)) * 4 + turned(a))
        for h in range(n_hi)
        for a in range(4)
        for b in range(4)
    ]

    def transpose(values):
        return lax.ppermute(values, AXES, to_rows)

    def shift_z(values, k):
        return lax.ppermute(values, "z", [(i, (i + k) % n_z) for i in range(n_z)])

    def gather_j(values):
        across = swap(values, "x")
        return [values, across, swap(values, "core"), swap(across, "core")]

    def cross_links(sent, kept):
        arrived = swap(sent, "core")
        half = kept.shape[0] // 2
        middle = (kept[half:] + arrived[half:].astype(F32)).astype(BF16)
        return kept, arrived, swap(middle, "x")

    def split_cols(full):
        n, total, cols = full.shape
        split = pick(full.reshape(n, total, 2, 4, cols // 8), j, 3)
        return split.transpose(1, 0, 2, 3).reshape(total, n * cols // 4)

    def split_rows(full):
        total, cols = full.shape
        return pick(full.reshape(2, 4, total // 8, cols), j, 1).reshape(total // 4, cols)

    def near_blocks(block):
        return [block] + [shift_z(block, -k) for k in range(1, n_z)]

    def after(values, *others):
        return lax.optimization_barrier((values, *others))[0]

    segs = transpose(jnp.concatenate([mem_seg.reshape(row_count, -1), dec_seg], 1))
    own_in = transpose(dec_in).reshape(own_tokens, width)
    tokens = gather_j(own_in)
    if fast:
        rows = proj_w.shape[1]
        cut = shaped((rows, 6 * local + ff_local), BF16)
        e = run(cut_cols_kernel, [proj_w, ffn_in], [cut] * 4)
        diag = [(0, 3), (1, 2), (2, 1), (3, 0)]
        e = [e[0], swap(e[1], "core"), swap(e[2], "x"), lax.ppermute(e[3], ("x", "core"), diag)]
        buf_a, buf_b, buf_c = run(
            pack_kernel,
            e + [out_w, ffn_out],
            [shaped((4, rows, width), BF16)] * 2 + [shaped((8, rows, ff_local), BF16)],
        )

        def placed(near, cols, row_rows, ffn):
            wcol, wrow = run(
                functools.partial(place_kernel, n_z, ffn),
                near + [swap(b, "hi") for b in near],
                [
                    shaped((2, 4, n_z, rows, cols), BF16),
                    shaped((2, n_z, row_rows, width), BF16),
                ],
            )
            return wcol.reshape(-1, cols), wrow.reshape(-1, width)

        near_a = near_blocks(buf_a)
        w_qkv, w_out = placed(near_a, 3 * local, rows, False)
        memory = after(memory, near_a[1])
        near_b = near_blocks(after(buf_b, near_a[1]))
        w_two, w_out2 = placed(near_b, 3 * local, rows, False)
        near_c = near_blocks(after(buf_c, near_b[1]))
        w_first, w_second = placed(near_c, ff_local, ffn_out.shape[0], True)
    else:
        proj_full = lax.all_gather(proj_w, AXES, axis=1, tiled=True)
        out_full = lax.all_gather(out_w, AXES, axis=1, tiled=True)
        w_qkv, w_two = split_cols(proj_full[:3]), split_cols(proj_full[3:])
        w_out, w_out2 = split_rows(out_full[0]), split_rows(out_full[1])
        w_first = split_cols(lax.all_gather(ffn_in, AXES, axis=0, tiled=True)[None])
        w_second = split_rows(lax.all_gather(ffn_out, AXES, axis=0, tiled=True))

    mems = gather_j(transpose(memory).reshape(row_count * slots, width))
    own_cot = transpose(after(cotangent, mems[1])).reshape(own_tokens, width)
    mem_full = mem_seg.shape[1] * mem_seg.shape[2]
    group = hi * 4 + turned(zi)
    own_dlen = lax.dynamic_slice_in_dim(dec_len, group * row_count, row_count)
    own_mlen = lax.dynamic_slice_in_dim(mem_len, group * row_count, row_count)
    parts = [turned(j ^ d) for d in ORDER]
    mem_parts = segs[:, :mem_full].reshape(row_count, tile_count, 4, tile_part)
    dec_parts = segs[:, mem_full:].reshape(row_count, 4, query_count)
    dseg = jnp.concatenate([pick(dec_parts, p, 1) for p in parts], 1)
    mseg = jnp.concatenate([pick(mem_parts, p, 2).reshape(row_count, slots) for p in parts], 1)
    dpos = jnp.concatenate([p * query_count + jnp.arange(query_count) for p in parts])
    in_tile = jnp.arange(tile_count)[:, None] * (4 * tile_part) + jnp.arange(tile_part)[None, :]
    mpos = jnp.concatenate([(in_tile + p * tile_part).reshape(-1) for p in parts])
    dlive = dpos[None, :] < own_dlen[:, None]
    mlive = mpos[None, :] < own_mlen[:, None]
    self_mask = (
        (dseg[:, :, None] == dseg[:, None, :])
        & (dpos[None, None, :] <= dpos[None, :, None])
        & dlive[:, None, :]
    ) | (dpos[None, None, :] == dpos[None, :, None])
    self_mask = self_mask.astype(F32)
    q_code = jnp.where(dlive, dseg.astype(F32), -2.0)[:, :, None]
    k_code = jnp.where(mlive, mseg.astype(F32), -1.0)[:, None, :]
    own_pos = parts[0] * query_count + jnp.arange(query_count)
    own_live = (own_pos[None, :] < own_dlen[:, None]).astype(F32).reshape(own_tokens, 1)
    bias_v2 = pick(biases[3].reshape(2, 4, width // 8), j, 1).reshape(local)
    bias_kv = jnp.concatenate([jnp.zeros((local,), F32), bias_v2])

    part = width // n_z // 2

    def sum_rep(kept, sent, cols):
        arrived = swap(sent, "hi")
        shape = kept.shape[1:]
        own, *out = run(
            pair_sum_kernel,
            [kept, arrived],
            [shaped(shape, F32)] + [shaped(shape, BF16)] * (n_z - 1),
        )
        arrived = [shift_z(block, i + 1) for i, block in enumerate(out)]
        return run(
            functools.partial(final_sum_kernel, cols),
            [own, *arrived],
            [shaped((shape[0], c), BF16) for c in cols],
        )

    to_plane = [
        ((h * 4 + 2 * a + b) * 4 + z, (b * 4 + z) * 4 + 2 * h + a)
        for h in range(2)
        for a in range(2)
        for b in range(2)
        for z in range(4)
    ]

    def gather_dp(block):
        pieces = [block, swap(block, "x")]
        pieces = pieces + [swap(p, "hi") for p in pieces]
        return [q for p in pieces for q in (p, swap(p, "core"))]

    def spread(blocks):
        return gather_dp(
            jnp.concatenate([blocks[0], lax.ppermute(blocks[1], AXES, to_plane)], 1)
        )

    def both(cols, rows=part):
        return [shaped((n_z, rows, cols), BF16)] * 2

    def tokens_scratch(cols):
        return pltpu.VMEM((all_tokens, cols), BF16)


    heads = shaped((4, row_count, query_count, local), BF16)
    sent = shaped((all_tokens // 2, width), BF16)
    kept = shaped((all_tokens // 2, width), F32)
    own_f32 = shaped((own_tokens, width), F32)
    own_low = shaped((own_tokens, width), BF16)
    rstd_shape = shaped((own_tokens, 128), F32)
    sums_shape = shaped((8, width), F32)
    qkv, mixed_self, s, k = run(
        self_fwd_kernel,
        [*tokens, w_qkv, w_out, biases, self_mask],
        [shaped((4, row_count, query_count, 3 * local), BF16), heads, sent, kept],
    )
    n_one, rstd_one, one_low = run(
        norm_one_kernel,
        [*cross_links(s, k), own_in, out_bias[None], norm_gain, norm_bias],
        [own_f32, rstd_shape, own_low],
    )
    ones = gather_j(one_low)
    w_kv2 = w_two[:, local:]
    kv2 = [(mm(m, w_kv2) + bias_kv).astype(BF16).reshape(row_count, slots, -1) for m in mems]
    query_two, mixed_cross, s, k = run(
        cross_fwd_kernel,
        [*ones, w_two, w_out2, biases, *kv2, q_code, k_code],
        [heads, heads, sent, kept],
    )
    n_two, rstd_two, two_low = run(
        norm_two_kernel,
        [*cross_links(s, k), n_one, biases, norm_gain, norm_bias],
        [own_f32, rstd_shape, own_low],
    )
    twos = gather_j(two_low)
    active, slope, s, k = run(
        ffn_fwd_kernel,
        [*twos, w_first, w_second, ffn_bias[None]],
        [shaped((all_tokens, ff_local), BF16), shaped((all_tokens, ff_local), F32), sent, kept],
    )
    mixed_out, d_three, own_f3, sums_three = run(
        norm_three_kernel,
        [*cross_links(s, k), n_two, biases, norm_gain, norm_bias, own_cot, own_live],
        [own_low, own_f32, own_low, sums_shape],
    )
    mixed_out = transpose(mixed_out.reshape(dec_in.shape))

    f3 = gather_j(own_f3)
    du, ff_sum, s, k = run(
        ffn_bwd_kernel,
        [*f3, w_first, w_second, slope],
        [shaped((all_tokens, ff_local), BF16), shaped((1, ff_local), F32), sent, kept],
    )
    k, arrived, crossed = cross_links(s, k)
    if fast:
        ffn_cols = (ff_local, width)
        kept_c, sent_c = run(
            functools.partial(ffn_grad_kernel, n_z),
            [*twos, du, active, *f3],
            both(sum(ffn_cols)),
            scratch=[tokens_scratch(width // 2), tokens_scratch(width)],
        )
        crossed = after(crossed, sent_c)
        ffn_gradients = run(
            ffn_out_kernel,
            spread(sum_rep(kept_c, sent_c, ffn_cols)),
            [shaped((width // n_z, ff_width), F32), shaped((ff_width // n_z, width), F32)],
        )

    d_two, own_f2, sums_two = run(
        functools.partial(norm_back_kernel, 1),
        [k, arrived, crossed, d_three, n_two, rstd_two, norm_gain],
        [own_f32, own_low, sums_shape],
    )
    f2 = gather_j(own_f2)
    memory_rows = shaped((row_count, slots, 2 * local), BF16)
    dq2, *dkv2, cross_sums, s, k = run(
        cross_bwd_kernel,
        [*f2, w_two, w_out2, query_two, *kv2, q_code, k_code],
        [heads] + [memory_rows] * 4 + [shaped((8, local), F32), sent, kept],
        scratch=[pltpu.VMEM(heads.shape, BF16)],
    )
    d_one, own_f1, sums_one = run(
        functools.partial(norm_back_kernel, 0),
        [*cross_links(s, k), d_two, n_one, rstd_one, norm_gain],
        [own_f32, own_low, sums_shape],
    )
    f1 = gather_j(own_f1)
    dqkv, sum_qkv, s, k = run(
        self_bwd_kernel,
        [*f1, w_qkv, w_out, qkv, self_mask],
        [
            shaped((4, row_count, query_count, 3 * local), BF16),
            shaped((1, 3 * local), F32),
            sent,
            kept,
        ],
    )
    k, arrived, crossed = cross_links(s, k)
    own_d = k[:own_tokens] + arrived[:own_tokens].astype(F32) + crossed.astype(F32) + d_one
    d_dec = transpose(own_d.astype(BF16).reshape(dec_in.shape)).astype(F32)

    flat_kv = [d.reshape(row_count * slots, -1) for d in dkv2]
    far = [swap(mm_t(d, w_kv2).astype(BF16), "core") for d in flat_kv[2:]]
    across = (mm_t(flat_kv[1], w_kv2) + far[1].astype(F32)).astype(BF16)
    near = mm_t(flat_kv[0], w_kv2) + far[0].astype(F32)
    d_memory = (near + swap(across, "x").astype(F32)).astype(BF16)
    d_memory = transpose(d_memory.reshape(memory.shape))

    ff_rows = ff_width // width
    n_small = -(-(11 + ff_rows) // 8) * 8
    small = run(
        small_kernel,
        [sums_three, sums_two, sums_one, cross_sums, ff_sum],
        shaped((n_small, width), F32),
    )
    if fast:
        for axis in ("core", "x", "hi"):
            small = small + swap(small, axis)
        for step in (1, 2):
            small = small + lax.ppermute(small, "z", [(i, i ^ step) for i in range(n_z)])
    else:
        small = lax.psum(small, AXES)

    dq2 = dq2.reshape(all_tokens, local)
    dqkv = dqkv.reshape(all_tokens, -1)
    o1 = mixed_self.reshape(all_tokens, local)
    o2 = mixed_cross.reshape(all_tokens, local)
    if fast:
        g_first, g_second = ffn_gradients

        def row_block(cols):
            return pl.BlockSpec((1, slots, cols), lambda r: (r, 0, 0))

        def fixed(array):
            return pl.BlockSpec(array.shape, lambda r: (0, 0, 0))

        outs = both(2 * local)
        kept_m, sent_m = pl.pallas_call(
            functools.partial(memory_grad_kernel, n_z),
            grid=(row_count,),
            in_specs=[row_block(width)] * 4 + [row_block(2 * local)] * 4,
            out_specs=[fixed(o) for o in outs],
            out_shape=outs,
            scratch_shapes=[
                pltpu.VMEM((4 * slots, width // 2), BF16),
                pltpu.VMEM((4 * slots, 2 * local), BF16),
                pltpu.VMEM((2, width // 2, 2 * local), F32),
            ],
            compiler_params=pltpu.CompilerParams(vmem_limit_bytes=VMEM_LIMIT),
        )(*[m.reshape(row_count, slots, width) for m in mems], *dkv2)
        kept_b, sent_b = run(
            functools.partial(cross_grad_kernel, n_z),
            [*ones, dq2, kept_m, sent_m, o2, *f2, o1, *f1],
            both(5 * local),
            scratch=[tokens_scratch(width // 2), tokens_scratch(width)],
        )
        g_proj, g_out = run(
            cross_out_kernel,
            spread(sum_rep(kept_b, sent_b, (3 * local, 2 * local))),
            [shaped((6, width // n_z, width), F32), shaped((2, width // n_z, width), F32)],
            scratch=[pltpu.VMEM((3, width // n_z, width), F32), pltpu.SemaphoreType.DMA],
            any_outs=(0,),
        )
        kept_a, sent_a = run(
            functools.partial(self_grad_kernel, n_z),
            [*tokens, dqkv, sum_qkv],
            both(3 * local, part + 16),
            scratch=[tokens_scratch(width // 2)],
        )
        g_proj, sums_qkv = run(
            self_out_kernel,
            gather_dp(sum_rep(kept_a, sent_a, (3 * local,))[0]) + [g_proj],
            [shaped(g_proj.shape, F32), shaped((8, width), F32)],
            scratch=[pltpu.VMEM((3, width // n_z, width), F32), pltpu.SemaphoreType.DMA],
            aliases={8: 0},
            any_args=(8,),
            any_outs=(0,),
        )
    else:
        mine = (jnp.arange(4) == j).astype(F32)[:, None]

        def col_grads(left, grads, n):
            cols = grads.shape[1] // n * 4
            total = t_mm(left, grads).reshape(-1, n, 2, 1, cols // 8)
            full = (total * mine).reshape(-1, n, cols).transpose(1, 0, 2)
            out = lax.psum_scatter(full.astype(BF16), "z", scatter_dimension=1, tiled=True)
            return lax.psum(out.astype(F32), ("hi", "x", "core"))

        def row_grads(left, grads):
            total = t_mm(left, grads).reshape(2, 1, -1, width)
            full = (total * mine[:, :, None]).reshape(-1, width)
            out = lax.psum_scatter(full.astype(BF16), "z", scatter_dimension=0, tiled=True)
            return lax.psum(out.astype(F32), ("hi", "x", "core"))

        def joined(pieces):
            return jnp.concatenate(pieces, 0)

        g_first = col_grads(joined(twos), du, 1)[0]
        g_second = row_grads(active, joined(f3))
        g_qkv = col_grads(joined(tokens), dqkv, 3)
        g_q2 = col_grads(joined(ones), dq2, 1)
        g_kv2 = col_grads(joined(mems), joined(flat_kv), 2)
        g_proj = jnp.concatenate([g_qkv, g_q2, g_kv2], 0)
        g_out = jnp.stack([row_grads(o1, joined(f1)), row_grads(o2, joined(f2))])
        sums_qkv = (sum_qkv.reshape(3, 2, 1, width // 8) * mine).reshape(3, width)
        sums_qkv = lax.psum(sums_qkv, AXES)

    n_part = width // n_z
    cut = lax.dynamic_slice_in_dim(small, zi * n_part, n_part, 1)
    cut_qkv = lax.dynamic_slice_in_dim(sums_qkv, zi * n_part, n_part, 1)
    g_biases = jnp.concatenate([cut_qkv[0:1], cut_qkv[2:3], cut[0:4]], 0)
    g_out_bias = cut[4]
    g_ffn_bias = lax.dynamic_slice_in_dim(
        small[5 : 5 + ff_rows].reshape(-1), zi * (ff_width // n_z), ff_width // n_z
    )
    g_gain = cut[5 + ff_rows : 8 + ff_rows]
    g_shift = cut[8 + ff_rows : 11 + ff_rows]
    return (
        mixed_out,
        d_dec,
        d_memory,
        g_proj,
        g_out,
        g_first,
        g_second,
        g_biases,
        g_out_bias,
        g_ffn_bias,
        g_gain,
        g_shift,
    )


def solution(mesh):
    devices = mesh.devices
    inner = Mesh(devices.reshape(devices.shape[0] // 4, 2, 2, devices.shape[1]), AXES)
    dp = ("hi", "x", "core")
    in_specs = (
        P(dp, "z", None),
        P(dp, None, "z", None),
        P(None, AXES, None),
        P(None, AXES, None),
        P(AXES, None),
        P(AXES, None),
        P(),
        P(),
        P(),
        P(),
        P(),
        P(),
        P(),
        P(dp, None, None),
        P(dp, None),
        P(dp, "z", None),
    )
    out_specs = (
        P(dp, "z", None),
        P(dp, "z", None),
        P(dp, None, "z", None),
        P(None, "z", None),
        P(None, "z", None),
        P("z", None),
        P("z", None),
        P(None, "z"),
        P("z"),
        P("z"),
        P(None, "z"),
        P(None, "z"),
    )
    return jax.shard_map(
        per_device, mesh=inner, in_specs=in_specs, out_specs=out_specs, check_vma=False
    )
```

time: 1890 us -> 644 us (0.34)
  the two profiles are of different devices: /device:TPU:2 before, /device:TPU:25 now
where the time goes in v1:
time: 644 us; the launch traced here: 634 us
  waiting for transfers between devices  276 us (43%)
  starting transfers between devices  162 us (25%)
  Pallas kernels  130 us (20%)
  matrix products  24.9 us (4%)
  local copies, waits for them, and re-layouts  21.1 us (3%)
  other arithmetic  19.2 us (3%)
    ppermute x77, waiting for transfers between devices, swap(): return lax.ppermute(values, axis, [(0, 1), (1, 0)])  127 us
    pallas_call x29, Pallas kernels, run(): pl.pallas_call(kernel, name=base.__name__, in_specs=[anywhere if i in any...  121 us
    ppermute x77, starting transfers between devices, swap(): return lax.ppermute(values, axis, [(0, 1), (1, 0)])  78.2 us
    ppermute x18, waiting for transfers between devices, shift_z(): return lax.ppermute(values, 'z', [(i, (i + k) % n_z) for i in range(n_z)])  67.9 us
    ppermute x7, waiting for transfers between devices, transpose(): return lax.ppermute(values, AXES, to_rows)  66 us
    ppermute x18, starting transfers between devices, shift_z(): return lax.ppermute(values, 'z', [(i, (i + k) % n_z) for i in range(n_z)])  45.8 us
    ppermute x7, starting transfers between devices, transpose(): return lax.ppermute(values, AXES, to_rows)  26.1 us
    unnamed x215, local copies, waits for them, and re-layouts  13.8 us
  transfers between devices with their start and end apart: 107, of which 44 were waited for; matrix products, arithmetic and copies ran while one was open for 8% of the time, Pallas kernels for 14%

profile of v1, /device:TPU:25, one launch (start us, length us, event | category | flops | bytes accessed | tf_op | source)
XLA Modules:
  0.0 634.3 jit_solution(976918374025347158)
XLA Ops:
  5.1 4.4 collective-permute-done.5.e2
  9.5 3.6 collective-permute-done.6.e3
  16.3 9.4 %collective-permute-done.7.refs_1_ = bf16[4,32,1024]{2,1,0:T(8,128)(2,1)S(1)} collective-permute-done((bf16[4,32,1024]{2,1,0:T(8,128)(2,1)}, bf16[4,32,1024]{2,1,0:T(8,128)(2,1)S(1)}, u32[]{:S(2)}, u32[]{:S(2)}) %collective-permute-start.7) | collective-permute-done | bytes 262176 | tf_op jit(solution)/shard_map/ppermute | solution.py:665
  27.7 4.3 collective-permute-start.14
  34.3 51.5 %collective-permute-done.14 = s32[3,1024]{1,0:T(4,128)S(1)} collective-permute-done((s32[3,1024]{1,0:T(4,128)S(1)}, s32[3,1024]{1,0:T(4,128)S(1)}, u32[]{:S(2)}, u32[]{:S(2)}) %collective-permute-start.14) | collective-permute-done | bytes 12320 | tf_op jit(solution)/shard_map/ppermute | solution.py:662
  89.4 4.3 collective-permute-done.1.x1
  103.8 4.1 collective-permute-done.12.refs_6_
  107.9 5.6 collective-permute-done.13.refs_7_
  113.5 3.0 place_kernel.3
  117.3 5.3 self_fwd_kernel.1
  129.1 4.7 collective-permute-done.20.refs_1_
  138.3 5.6 collective-permute-done.21.refs_2_
  159.3 3.6 collective-permute-done.26.refs_7_
  162.9 3.0 place_kernel.4
  168.6 3.1 fusion
  171.6 3.1 fusion.1
  174.7 3.1 fusion.2
  177.8 3.1 fusion.3
  181.6 9.5 %cross_fwd_kernel.1 = (bf16[4,3,32,256]{3,2,1,0:T(8,128)(2,1)}, bf16[4,3,32,256]{3,2,1,0:T(8,128)(2,1)}, bf16[192,1024]{1,0:T(8,128)(2,1)}, f32[192,1024]{1,0:T(8,128)}) custom-call(bf16[96,1024]{1,0:T(8,128)(2,1)} %get-tuple-element.113.h0, bf16[96,1024]{1,0:T(8,128)(2,1)} %copy-done.15, bf16[96,1024]{1,0:T(8,128)(2,1)} %copy-done.16, ...), custom_call_target="tpu_custom_call" | custom-call | tf_op jit(solution)/shard_map/cross_fwd_kernel/pallas_call | solution.py:109
  191.6 4.4 collective-permute-start.36
  202.2 8.4 %collective-permute-done.36.refs_1_ = bf16[8,32,1024]{2,1,0:T(8,128)(2,1)S(1)} collective-permute-done((bf16[8,32,1024]{2,1,0:T(8,128)(2,1)S(1)}, bf16[8,32,1024]{2,1,0:T(8,128)(2,1)S(1)}, u32[]{:S(2)}, u32[]{:S(2)}) %collective-permute-start.36) | collective-permute-done | bytes 524320 | tf_op jit(solution)/shard_map/ppermute | solution.py:665
  211.9 21.4 %collective-permute-done.37.refs_2_ = bf16[8,32,1024]{2,1,0:T(8,128)(2,1)S(1)} collective-permute-done((bf16[8,32,1024]{2,1,0:T(8,128)(2,1)S(1)}, bf16[8,32,1024]{2,1,0:T(8,128)(2,1)S(1)}, u32[]{:S(2)}, u32[]{:S(2)}) %collective-permute-start.37) | collective-permute-done | bytes 524320 | tf_op jit(solution)/shard_map/ppermute | solution.py:665
  240.2 3.4 collective-permute-done.33.h1.a1
  246.4 11.2 %collective-permute-done.42.refs_7_ = bf16[8,32,1024]{2,1,0:T(8,128)(2,1)} collective-permute-done((bf16[8,32,1024]{2,1,0:T(8,128)(2,1)S(1)}, bf16[8,32,1024]{2,1,0:T(8,128)(2,1)}, u32[]{:S(2)}, u32[]{:S(2)}) %collective-permute-start.42) | collective-permute-done | bytes 524320 | tf_op jit(solution)/shard_map/ppermute | solution.py:40
  257.7 4.4 place_kernel.5
  262.9 5.9 ffn_fwd_kernel.1
  270.1 10.7 %collective-permute-start.45 = (bf16[3,32,1024]{2,1,0:T(8,128)(2,1)S(1)}, bf16[3,32,1024]{2,1,0:T(8,128)(2,1)S(1)}, u32[]{:S(2)}, u32[]{:S(2)}) collective-permute-start(bf16[3,32,1024]{2,1,0:T(8,128)(2,1)S(1)} %copy-done.100), channel_id=1, source_target_pairs={{0,0},{1,8},{2,4},{3,12},{4,2},{5,10},{6,6},{7,14},{8,1},{9,9},{10... | collective-permute-start | bytes 589832 | tf_op jit(solution)/shard_map/ppermute | solution.py:662
  284.6 4.7 collective-permute-done.44.crossed
  297.6 3.4 collective-permute-start.49
  302.8 6.2 ffn_bwd_kernel.1
  312.2 5.8 ffn_grad_kernel.1
  323.8 3.3 collective-permute-done.52.f1.f21
  331.0 11.8 %cross_bwd_kernel.1 = (bf16[4,3,32,256]{3,2,1,0:T(8,128)(2,1)}, bf16[3,224,512]{2,1,0:T(8,128)(2,1)}, bf16[3,224,512]{2,1,0:T(8,128)(2,1)}, bf16[3,224,512]{2,1,...) custom-call(bf16[96,1024]{1,0:T(8,128)(2,1)} %get-tuple-element.142., ...), custom_call_target="tpu_custom_call" | custom-call | tf_op jit(solution)/shard_map/cross_bwd_kernel/pallas_call | solution.py:109
  343.9 3.2 convolution_convert_fusion.1
  351.2 3.0 collective-permute-done.56.crossed
  363.6 3.1 collective-permute-done.103
  370.6 6.3 self_bwd_kernel.1
  377.5 14.5 %collective-permute-done.104 = f32[16,1024]{1,0:T(8,128)} collective-permute-done((f32[16,1024]{1,0:T(8,128)S(1)}, f32[16,1024]{1,0:T(8,128)}, u32[]{:S(2)}, u32[]{:S(2)}) %collective-permute-start.104) | collective-permute-done | bytes 65568 | tf_op jit(solution)/shard_map/ppermute | solution.py:40
  397.3 3.4 collective-permute-start.46
  400.7 8.4 %collective-permute-done.46 = bf16[3,32,1024]{2,1,0:T(8,128)(2,1)} collective-permute-done((bf16[3,32,1024]{2,1,0:T(8,128)(2,1)}, bf16[3,32,1024]{2,1,0:T(8,128)(2,1)}, u32[]{:S(2)}, u32[]{:S(2)}) %collective-permute-start.46) | collective-permute-done | bytes 196640 | tf_op jit(solution)/shard_map/ppermute | solution.py:662
  409.1 3.7 collective-permute-start.106
  412.8 8.7 %shard_map.247 = (bf16[4,128,512]{2,1,0:T(8,128)(2,1)}, bf16[4,128,512]{2,1,0:T(8,128)(2,1)}) custom-call(bf16[3,224,1024]{2,1,0:T(8,128)(2,1)} %bitcast.98, bf16[3,224,1024]{2,1,0:T(8,128)(2,1)} %bitcast.31.refs_1_, bf16[3,224,1024]{2,1,0:T(8,128)(2,1)} %bitcast.32.refs_2_, bf16[3,224,1024]{2,1,0:T(8,128)(2,1)} %bitcast.33.refs_3_, ...), custom_call_target="tpu_custom_call" | custom-call | tf_op jit(solution)/shard_map/pallas_call | solution.py:938
  421.5 3.8 self_grad_kernel.1
  425.3 4.8 cross_grad_kernel.1
  434.7 3.9 pair_sum_kernel.5
  440.1 3.6 add_convert_fusion.1
  443.7 7.6 %collective-permute-done.91.refs_0_ = bf16[128,2048]{1,0:T(8,128)(2,1)S(1)} collective-permute-done((bf16[128,2048]{1,0:T(8,128)(2,1)}, bf16[128,2048]{1,0:T(8,128)(2,1)S(1)}, u32[]{:S(2)}, u32[]{:S(2)}) %collective-permute-start.91) | collective-permute-done | bytes 524320 | tf_op jit(solution)/shard_map/ppermute | solution.py:665
  453.2 25.1 %collective-permute-done.67.arrived = bf16[4,144,768]{2,1,0:T(8,128)(2,1)} collective-permute-done((bf16[4,144,768]{2,1,0:T(8,128)(2,1)}, bf16[4,144,768]{2,1,0:T(8,128)(2,1)}, u32[]{:S(2)}, u32[]{:S(2)}) %collective-permute-start.67) | collective-permute-done | bytes 884768 | tf_op jit(solution)/shard_map/ppermute | solution.py:40
  482.8 6.9 %collective-permute-start.68 = (bf16[144,768]{1,0:T(8,128)(2,1)}, bf16[144,768]{1,0:T(8,128)(2,1)S(1)}, u32[]{:S(2)}, u32[]{:S(2)}) collective-permute-start(bf16[144,768]{1,0:T(8,128)(2,1)} %get-tuple-element.162), channel_id=1, source_target_pairs={{0,1},{1,2},{2,3},{3,0},{4,5},{5,6},{6,7},{7,4},{8,9},{9,10},{10,1... | collective-permute-start | bytes 663560 | tf_op jit(solution)/shard_map/ppermute | solution.py:665
  497.7 3.0 pair_sum_kernel.4
  500.7 9.5 %collective-permute-start.79 = (bf16[128,1280]{1,0:T(8,128)(2,1)}, bf16[128,1280]{1,0:T(8,128)(2,1)S(1)}, u32[]{:S(2)}, u32[]{:S(2)}) collective-permute-start(bf16[128,1280]{1,0:T(8,128)(2,1)} %get-tuple-element.173), channel_id=1, source_target_pairs={{0,1},{1,2},{2,3},{3,0},{4,5},{5,6},{6,7},{7,4},{8,9},{9,10},{10,1... | collective-permute-start | bytes 983048 | tf_op jit(solution)/shard_map/ppermute | solution.py:665
  510.9 16.8 %collective-permute-start.81 = (bf16[128,1280]{1,0:T(8,128)(2,1)}, bf16[128,1280]{1,0:T(8,128)(2,1)}, u32[]{:S(2)}, u32[]{:S(2)}) collective-permute-start(bf16[128,1280]{1,0:T(8,128)(2,1)} %get-tuple-element.175), channel_id=1, source_target_pairs={{0,3},{1,0},{2,1},{3,2},{4,7},{5,4},{6,5},{7,6},{8,11},{9,8},{10,9... | collective-permute-start | bytes 983048 | tf_op jit(solution)/shard_map/ppermute | solution.py:665
  531.5 8.8 %collective-permute-done.80.refs_1_ = bf16[128,1280]{1,0:T(8,128)(2,1)} collective-permute-done((bf16[128,1280]{1,0:T(8,128)(2,1)}, bf16[128,1280]{1,0:T(8,128)(2,1)}, u32[]{:S(2)}, u32[]{:S(2)}) %collective-permute-start.80) | collective-permute-done | bytes 327712 | tf_op jit(solution)/shard_map/ppermute | solution.py:665
  540.3 10.6 %collective-permute-start.98 = (bf16[128,2048]{1,0:T(8,128)(2,1)S(1)}, bf16[128,2048]{1,0:T(8,128)(2,1)}, u32[]{:S(2)}, u32[]{:S(2)}) collective-permute-start(bf16[128,2048]{1,0:T(8,128)(2,1)S(1)} %constant_dynamic-update-slice_fusion.2.refs_0_), channel_id=1, source_target_pairs={{0,16},{16,0},{1,17},{17,1},{2,18},{18,2},{3,19},{19,3},{4,20},{20... | collective-permute-start | bytes 1572872 | tf_op jit(solution)/shard_map/ppermute | solution.py:40
  555.0 9.9 %collective-permute-done.82 = bf16[128,512]{1,0:T(8,128)(2,1)S(1)} collective-permute-done((bf16[128,512]{1,0:T(8,128)(2,1)}, bf16[128,512]{1,0:T(8,128)(2,1)S(1)}, u32[]{:S(2)}, u32[]{:S(2)}) %collective-permute-start.82) | collective-permute-done | bytes 131104 | tf_op jit(solution)/shard_map/ppermute | solution.py:794
  566.0 6.3 collective-permute-done.74.refs_4_
  574.8 3.8 add_convert_fusion
  581.0 9.4 %collective-permute-done.100.refs_6_ = bf16[128,2048]{1,0:T(8,128)(2,1)} collective-permute-done((bf16[128,2048]{1,0:T(8,128)(2,1)S(1)}, bf16[128,2048]{1,0:T(8,128)(2,1)}, u32[]{:S(2)}, u32[]{:S(2)}) %collective-permute-start.100) | collective-permute-done | bytes 524320 | tf_op jit(solution)/shard_map/ppermute | solution.py:40
  593.9 4.5 collective-permute-done.86.refs_4_
  598.4 3.9 collective-permute-start.85
  602.4 3.1 collective-permute-done.88.refs_6_
  613.2 6.1 ffn_out_kernel.1
  619.3 5.2 cross_out_kernel.1
  625.5 4.2 self_out_kernel.1
  (460 shorter events, 177.8 us)
Async XLA Ops:
  25.7 69.3 %collective-permute-start.27 = (bf16[3,7,32,1024]{3,2,1,0:T(8,128)(2,1)}, bf16[3,7,32,1024]{3,2,1,0:T(8,128)(2,1)S(1)}, u32[]{:S(2)}, u32[]{:S(2)}) collective-permute-start(bf16[3,7,32,1024]{3,2,1,0:T(8,128)(2,1)} %param.17), channel_id=1, source_target_pairs={{0,0},{1,8},{2,4},{3,12},{4,2},{5,10},{6,6},{7,14},{8,1},{9,9},{10... | collective-permute-start | bytes 4128776 | tf_op jit(solution)/shard_map/ppermute | solution.py:662
  27.7 58.0 %collective-permute-start.14 = (s32[3,1024]{1,0:T(4,128)S(1)}, s32[3,1024]{1,0:T(4,128)S(1)}, u32[]{:S(2)}, u32[]{:S(2)}) collective-permute-start(s32[3,1024]{1,0:T(4,128)S(1)} %pad_add_fusion), channel_id=1, source_target_pairs={{0,0},{1,8},{2,4},{3,12},{4,2},{5,10},{6,6},{7,14},{8,1},{9,9},{10... | collective-permute-start | bytes 36872 | tf_op jit(solution)/shard_map/ppermute | solution.py:662
  31.9 56.2 %collective-permute-start = (bf16[3,32,1024]{2,1,0:T(8,128)(2,1)S(1)}, bf16[3,32,1024]{2,1,0:T(8,128)(2,1)S(1)}, u32[]{:S(2)}, u32[]{:S(2)}) collective-permute-start(bf16[3,32,1024]{2,1,0:T(8,128)(2,1)S(1)} %copy-done.99), channel_id=1, source_target_pairs={{0,0},{1,8},{2,4},{3,12},{4,2},{5,10},{6,6},{7,14},{8,1},{9,9},{10... | collective-permute-start | bytes 589832 | tf_op jit(solution)/shard_map/ppermute | solution.py:662
  95.0 55.3 %collective-permute-start.28 = (bf16[672,1024]{1,0:T(8,128)(2,1)S(1)}, bf16[672,1024]{1,0:T(8,128)(2,1)}, u32[]{:S(2)}, u32[]{:S(2)}) collective-permute-start(bf16[672,1024]{1,0:T(8,128)(2,1)S(1)} %bitcast.95), channel_id=1, source_target_pairs={{0,8},{8,0},{1,9},{9,1},{2,10},{10,2},{3,11},{11,3},{4,12},{12,4},... | collective-permute-start | bytes 4128776 | tf_op jit(solution)/shard_map/ppermute | solution.py:40
  97.5 15.9 %collective-permute-start.13 = (bf16[4,32,1024]{2,1,0:T(8,128)(2,1)S(1)}, bf16[4,32,1024]{2,1,0:T(8,128)(2,1)}, u32[]{:S(2)}, u32[]{:S(2)}) collective-permute-start(bf16[4,32,1024]{2,1,0:T(8,128)(2,1)S(1)} %collective-permute-done.9.refs_3_), channel_id=1, source_target_pairs={{0,16},{16,0},{1,17},{17,1},{2,18},{18,2},{3,19},{19,3},{4,20},{20... | collective-permute-start | bytes 786440 | tf_op jit(solution)/shard_map/ppermute | solution.py:40
  98.9 17.6 %collective-permute-start.2 = (bf16[96,1024]{1,0:T(8,128)(2,1)S(1)}, bf16[96,1024]{1,0:T(8,128)(2,1)S(1)}, u32[]{:S(2)}, u32[]{:S(2)}) collective-permute-start(bf16[96,1024]{1,0:T(8,128)(2,1)S(1)} %bitcast.91), channel_id=1, source_target_pairs={{0,4},{4,0},{1,5},{5,1},{2,6},{6,2},{3,7},{7,3},{8,12},{12,8},{9,1... | collective-permute-start | bytes 589832 | tf_op jit(solution)/shard_map/ppermute | solution.py:40
  102.2 14.3 %collective-permute-start.3 = (bf16[96,1024]{1,0:T(8,128)(2,1)S(1)}, bf16[96,1024]{1,0:T(8,128)(2,1)S(1)}, u32[]{:S(2)}, u32[]{:S(2)}) collective-permute-start(bf16[96,1024]{1,0:T(8,128)(2,1)S(1)} %collective-permute-done.1.x1), channel_id=1, source_target_pairs={{0,4},{4,0},{1,5},{5,1},{2,6},{6,2},{3,7},{7,3},{8,12},{12,8},{9,1... | collective-permute-start | bytes 589832 | tf_op jit(solution)/shard_map/ppermute | solution.py:40
  122.6 12.5 %collective-permute-start.15 = (bf16[192,1024]{1,0:T(8,128)(2,1)}, bf16[192,1024]{1,0:T(8,128)(2,1)S(1)}, u32[]{:S(2)}, u32[]{:S(2)}) collective-permute-start(bf16[192,1024]{1,0:T(8,128)(2,1)} %get-tuple-element.112), channel_id=1, source_target_pairs={{0,4},{4,0},{1,5},{5,1},{2,6},{6,2},{3,7},{7,3},{8,12},{12,8},{9,1... | collective-permute-start | bytes 1179656 | tf_op jit(solution)/shard_map/ppermute | solution.py:40
  124.1 19.8 %collective-permute-start.21 = (bf16[4,32,1024]{2,1,0:T(8,128)(2,1)S(1)}, bf16[4,32,1024]{2,1,0:T(8,128)(2,1)S(1)}, u32[]{:S(2)}, u32[]{:S(2)}) collective-permute-start(bf16[4,32,1024]{2,1,0:T(8,128)(2,1)S(1)} %copy-done.55), channel_id=1, source_target_pairs={{0,2},{1,3},{2,0},{3,1},{4,6},{5,7},{6,4},{7,5},{8,10},{9,11},{10,... | collective-permute-start | bytes 786440 | tf_op jit(solution)/shard_map/ppermute | solution.py:665
  127.3 18.0 %collective-permute-start.22 = (bf16[4,32,1024]{2,1,0:T(8,128)(2,1)S(1)}, bf16[4,32,1024]{2,1,0:T(8,128)(2,1)S(1)}, u32[]{:S(2)}, u32[]{:S(2)}) collective-permute-start(bf16[4,32,1024]{2,1,0:T(8,128)(2,1)S(1)} %copy-done.55), channel_id=1, source_target_pairs={{0,1},{1,2},{2,3},{3,0},{4,5},{5,6},{6,7},{7,4},{8,9},{9,10},{10,1... | collective-permute-start | bytes 786440 | tf_op jit(solution)/shard_map/ppermute | solution.py:665
  133.8 14.9 %collective-permute-start.23 = (bf16[4,32,1024]{2,1,0:T(8,128)(2,1)S(1)}, bf16[4,32,1024]{2,1,0:T(8,128)(2,1)S(1)}, u32[]{:S(2)}, u32[]{:S(2)}) collective-permute-start(bf16[4,32,1024]{2,1,0:T(8,128)(2,1)S(1)} %copy-done.55), channel_id=1, source_target_pairs={{0,16},{16,0},{1,17},{17,1},{2,18},{18,2},{3,19},{19,3},{4,20},{20... | collective-permute-start | bytes 786440 | tf_op jit(solution)/shard_map/ppermute | solution.py:40
  135.1 39.7 %collective-permute-start.29 = (bf16[672,1024]{1,0:T(8,128)(2,1)S(1)}, bf16[672,1024]{1,0:T(8,128)(2,1)}, u32[]{:S(2)}, u32[]{:S(2)}) collective-permute-start(bf16[672,1024]{1,0:T(8,128)(2,1)S(1)} %bitcast.96), channel_id=1, source_target_pairs={{0,4},{4,0},{1,5},{5,1},{2,6},{6,2},{3,7},{7,3},{8,12},{12,8},{9,1... | collective-permute-start | bytes 4128776 | tf_op jit(solution)/shard_map/ppermute | solution.py:40
  145.3 12.4 %collective-permute-start.24 = (bf16[4,32,1024]{2,1,0:T(8,128)(2,1)S(1)}, bf16[4,32,1024]{2,1,0:T(8,128)(2,1)S(1)}, u32[]{:S(2)}, u32[]{:S(2)}) collective-permute-start(bf16[4,32,1024]{2,1,0:T(8,128)(2,1)S(1)} %collective-permute-done.20.refs_1_), channel_id=1, source_target_pairs={{0,16},{16,0},{1,17},{17,1},{2,18},{18,2},{3,19},{19,3},{4,20},{20... | collective-permute-start | bytes 786440 | tf_op jit(solution)/shard_map/ppermute | solution.py:40
  149.1 13.8 %collective-permute-start.26 = (bf16[4,32,1024]{2,1,0:T(8,128)(2,1)S(1)}, bf16[4,32,1024]{2,1,0:T(8,128)(2,1)}, u32[]{:S(2)}, u32[]{:S(2)}) collective-permute-start(bf16[4,32,1024]{2,1,0:T(8,128)(2,1)S(1)} %collective-permute-done.22.refs_3_), channel_id=1, source_target_pairs={{0,16},{16,0},{1,17},{17,1},{2,18},{18,2},{3,19},{19,3},{4,20},{20... | collective-permute-start | bytes 786440 | tf_op jit(solution)/shard_map/ppermute | solution.py:40
  150.3 27.5 %collective-permute-start.30 = (bf16[672,1024]{1,0:T(8,128)(2,1)}, bf16[672,1024]{1,0:T(8,128)(2,1)}, u32[]{:S(2)}, u32[]{:S(2)}) collective-permute-start(bf16[672,1024]{1,0:T(8,128)(2,1)} %collective-permute-done.28), channel_id=1, source_target_pairs={{0,4},{4,0},{1,5},{5,1},{2,6},{6,2},{3,7},{7,3},{8,12},{12,8},{9,1... | collective-permute-start | bytes 4128776 | tf_op jit(solution)/shard_map/ppermute | solution.py:40
  165.9 15.0 %collective-permute-start.18 = (bf16[96,1024]{1,0:T(8,128)(2,1)S(1)}, bf16[96,1024]{1,0:T(8,128)(2,1)S(1)}, u32[]{:S(2)}, u32[]{:S(2)}) collective-permute-start(bf16[96,1024]{1,0:T(8,128)(2,1)S(1)} %copy-done.14), channel_id=1, source_target_pairs={{0,4},{4,0},{1,5},{5,1},{2,6},{6,2},{3,7},{7,3},{8,12},{12,8},{9,1... | collective-permute-start | bytes 589832 | tf_op jit(solution)/shard_map/ppermute | solution.py:40
  168.5 12.4 %collective-permute-start.19 = (bf16[96,1024]{1,0:T(8,128)(2,1)S(1)}, bf16[96,1024]{1,0:T(8,128)(2,1)S(1)}, u32[]{:S(2)}, u32[]{:S(2)}) collective-permute-start(bf16[96,1024]{1,0:T(8,128)(2,1)S(1)} %collective-permute-done.17.h1), channel_id=1, source_target_pairs={{0,4},{4,0},{1,5},{5,1},{2,6},{6,2},{3,7},{7,3},{8,12},{12,8},{9,1... | collective-permute-start | bytes 589832 | tf_op jit(solution)/shard_map/ppermute | solution.py:40
  191.6 19.1 %collective-permute-start.36 = (bf16[8,32,1024]{2,1,0:T(8,128)(2,1)S(1)}, bf16[8,32,1024]{2,1,0:T(8,128)(2,1)S(1)}, u32[]{:S(2)}, u32[]{:S(2)}) collective-permute-start(bf16[8,32,1024]{2,1,0:T(8,128)(2,1)S(1)} %copy-done.39), channel_id=1, source_target_pairs={{0,3},{1,0},{2,1},{3,2},{4,7},{5,4},{6,5},{7,6},{8,11},{9,8},{10,9... | collective-permute-start | bytes 1572872 | tf_op jit(solution)/shard_map/ppermute | solution.py:665
  196.0 37.3 %collective-permute-start.37 = (bf16[8,32,1024]{2,1,0:T(8,128)(2,1)S(1)}, bf16[8,32,1024]{2,1,0:T(8,128)(2,1)S(1)}, u32[]{:S(2)}, u32[]{:S(2)}) collective-permute-start(bf16[8,32,1024]{2,1,0:T(8,128)(2,1)S(1)} %copy-done.39), channel_id=1, source_target_pairs={{0,2},{1,3},{2,0},{3,1},{4,6},{5,7},{6,4},{7,5},{8,10},{9,11},{10,... | collective-permute-start | bytes 1572872 | tf_op jit(solution)/shard_map/ppermute | solution.py:665
  198.6 35.9 %collective-permute-start.38 = (bf16[8,32,1024]{2,1,0:T(8,128)(2,1)S(1)}, bf16[8,32,1024]{2,1,0:T(8,128)(2,1)S(1)}, u32[]{:S(2)}, u32[]{:S(2)}) collective-permute-start(bf16[8,32,1024]{2,1,0:T(8,128)(2,1)S(1)} %copy-done.39), channel_id=1, source_target_pairs={{0,1},{1,2},{2,3},{3,0},{4,5},{5,6},{6,7},{7,4},{8,9},{9,10},{10,1... | collective-permute-start | bytes 1572872 | tf_op jit(solution)/shard_map/ppermute | solution.py:665
  198.8 40.1 %collective-permute-start.39 = (bf16[8,32,1024]{2,1,0:T(8,128)(2,1)S(1)}, bf16[8,32,1024]{2,1,0:T(8,128)(2,1)S(1)}, u32[]{:S(2)}, u32[]{:S(2)}) collective-permute-start(bf16[8,32,1024]{2,1,0:T(8,128)(2,1)S(1)} %copy-done.39), channel_id=1, source_target_pairs={{0,16},{16,0},{1,17},{17,1},{2,18},{18,2},{3,19},{19,3},{4,20},{20... | collective-permute-start | bytes 1572872 | tf_op jit(solution)/shard_map/ppermute | solution.py:40
  201.3 33.5 %collective-permute-start.32 = (bf16[96,1024]{1,0:T(8,128)(2,1)S(1)}, bf16[96,1024]{1,0:T(8,128)(2,1)S(1)}, u32[]{:S(2)}, u32[]{:S(2)}) collective-permute-start(bf16[96,1024]{1,0:T(8,128)(2,1)S(1)} %add_convert_fusion.7), channel_id=1, source_target_pairs={{0,8},{8,0},{1,9},{9,1},{2,10},{10,2},{3,11},{11,3},{4,12},{12,4},... | collective-permute-start | bytes 589832 | tf_op jit(solution)/shard_map/ppermute | solution.py:40
  210.6 34.9 %collective-permute-start.40 = (bf16[8,32,1024]{2,1,0:T(8,128)(2,1)S(1)}, bf16[8,32,1024]{2,1,0:T(8,128)(2,1)S(1)}, u32[]{:S(2)}, u32[]{:S(2)}) collective-permute-start(bf16[8,32,1024]{2,1,0:T(8,128)(2,1)S(1)} %collective-permute-done.36.refs_1_), channel_id=1, source_target_pairs={{0,16},{16,0},{1,17},{17,1},{2,18},{18,2},{3,19},{19,3},{4,20},{20... | collective-permute-start | bytes 1572872 | tf_op jit(solution)/shard_map/ppermute | solution.py:40
  233.3 13.1 %collective-permute-start.41 = (bf16[8,32,1024]{2,1,0:T(8,128)(2,1)S(1)}, bf16[8,32,1024]{2,1,0:T(8,128)(2,1)}, u32[]{:S(2)}, u32[]{:S(2)}) collective-permute-start(bf16[8,32,1024]{2,1,0:T(8,128)(2,1)S(1)} %collective-permute-done.37.refs_2_), channel_id=1, source_target_pairs={{0,16},{16,0},{1,17},{17,1},{2,18},{18,2},{3,19},{19,3},{4,20},{20... | collective-permute-start | bytes 1572872 | tf_op jit(solution)/shard_map/ppermute | solution.py:40
  234.5 23.1 %collective-permute-start.42 = (bf16[8,32,1024]{2,1,0:T(8,128)(2,1)S(1)}, bf16[8,32,1024]{2,1,0:T(8,128)(2,1)}, u32[]{:S(2)}, u32[]{:S(2)}) collective-permute-start(bf16[8,32,1024]{2,1,0:T(8,128)(2,1)S(1)} %collective-permute-done.38.refs_3_), channel_id=1, source_target_pairs={{0,16},{16,0},{1,17},{17,1},{2,18},{18,2},{3,19},{19,3},{4,20},{20... | collective-permute-start | bytes 1572872 | tf_op jit(solution)/shard_map/ppermute | solution.py:40
  238.9 23.2 %collective-permute-start.34 = (bf16[96,1024]{1,0:T(8,128)(2,1)}, bf16[96,1024]{1,0:T(8,128)(2,1)S(1)}, u32[]{:S(2)}, u32[]{:S(2)}) collective-permute-start(bf16[96,1024]{1,0:T(8,128)(2,1)} %get-tuple-element.122.h0.a0), channel_id=1, source_target_pairs={{0,4},{4,0},{1,5},{5,1},{2,6},{6,2},{3,7},{7,3},{8,12},{12,8},{9,1... | collective-permute-start | bytes 589832 | tf_op jit(solution)/shard_map/ppermute | solution.py:40
  243.7 18.4 %collective-permute-start.35 = (bf16[96,1024]{1,0:T(8,128)(2,1)S(1)}, bf16[96,1024]{1,0:T(8,128)(2,1)S(1)}, u32[]{:S(2)}, u32[]{:S(2)}) collective-permute-start(bf16[96,1024]{1,0:T(8,128)(2,1)S(1)} %collective-permute-done.33.h1.a1), channel_id=1, source_target_pairs={{0,4},{4,0},{1,5},{5,1},{2,6},{6,2},{3,7},{7,3},{8,12},{12,8},{9,1... | collective-permute-start | bytes 589832 | tf_op jit(solution)/shard_map/ppermute | solution.py:40
  268.8 12.1 %collective-permute-start.43 = (bf16[192,1024]{1,0:T(8,128)(2,1)}, bf16[192,1024]{1,0:T(8,128)(2,1)S(1)}, u32[]{:S(2)}, u32[]{:S(2)}) collective-permute-start(bf16[192,1024]{1,0:T(8,128)(2,1)} %get-tuple-element.128), channel_id=1, source_target_pairs={{0,4},{4,0},{1,5},{5,1},{2,6},{6,2},{3,7},{7,3},{8,12},{12,8},{9,1... | collective-permute-start | bytes 1179656 | tf_op jit(solution)/shard_map/ppermute | solution.py:40
  270.1 14.5 %collective-permute-start.45 = (bf16[3,32,1024]{2,1,0:T(8,128)(2,1)S(1)}, bf16[3,32,1024]{2,1,0:T(8,128)(2,1)S(1)}, u32[]{:S(2)}, u32[]{:S(2)}) collective-permute-start(bf16[3,32,1024]{2,1,0:T(8,128)(2,1)S(1)} %copy-done.100), channel_id=1, source_target_pairs={{0,0},{1,8},{2,4},{3,12},{4,2},{5,10},{6,6},{7,14},{8,1},{9,9},{10... | collective-permute-start | bytes 589832 | tf_op jit(solution)/shard_map/ppermute | solution.py:662
  343.2 90.2 %collective-permute-start.90 = (bf16[4,128,2048]{2,1,0:T(8,128)(2,1)}, bf16[4,128,2048]{2,1,0:T(8,128)(2,1)S(1)}, u32[]{:S(2)}, u32[]{:S(2)}) collective-permute-start(bf16[4,128,2048]{2,1,0:T(8,128)(2,1)} %get-tuple-element.138), channel_id=1, source_target_pairs={{0,16},{16,0},{1,17},{17,1},{2,18},{18,2},{3,19},{19,3},{4,20},{20... | collective-permute-start | bytes 6291464 | tf_op jit(solution)/shard_map/ppermute | solution.py:40
  347.1 91.4 %collective-permute-start.63 = (bf16[672,1024]{1,0:T(8,128)(2,1)}, bf16[672,1024]{1,0:T(8,128)(2,1)}, u32[]{:S(2)}, u32[]{:S(2)}) collective-permute-start(bf16[672,1024]{1,0:T(8,128)(2,1)} %convolution_convert_fusion.1), channel_id=1, source_target_pairs={{0,4},{4,0},{1,5},{5,1},{2,6},{6,2},{3,7},{7,3},{8,12},{12,8},{9,1... | collective-permute-start | bytes 4128776 | tf_op jit(solution)/shard_map/ppermute | solution.py:40
  350.8 87.7 %collective-permute-start.64 = (bf16[672,1024]{1,0:T(8,128)(2,1)}, bf16[672,1024]{1,0:T(8,128)(2,1)}, u32[]{:S(2)}, u32[]{:S(2)}) collective-permute-start(bf16[672,1024]{1,0:T(8,128)(2,1)} %convolution_convert_fusion), channel_id=1, source_target_pairs={{0,4},{4,0},{1,5},{5,1},{2,6},{6,2},{3,7},{7,3},{8,12},{12,8},{9,1... | collective-permute-start | bytes 4128776 | tf_op jit(solution)/shard_map/ppermute | solution.py:40
  369.2 22.8 %collective-permute-start.104 = (f32[16,1024]{1,0:T(8,128)S(1)}, f32[16,1024]{1,0:T(8,128)}, u32[]{:S(2)}, u32[]{:S(2)}) collective-permute-start(f32[16,1024]{1,0:T(8,128)S(1)} %add.294), channel_id=1, source_target_pairs={{0,16},{16,0},{1,17},{17,1},{2,18},{18,2},{3,19},{19,3},{4,20},{20... | collective-permute-start | bytes 196616 | tf_op jit(solution)/shard_map/ppermute | solution.py:40
  376.9 54.0 %collective-permute-start.60 = (bf16[192,1024]{1,0:T(8,128)(2,1)}, bf16[192,1024]{1,0:T(8,128)(2,1)S(1)}, u32[]{:S(2)}, u32[]{:S(2)}) collective-permute-start(bf16[192,1024]{1,0:T(8,128)(2,1)} %get-tuple-element.151), channel_id=1, source_target_pairs={{0,4},{4,0},{1,5},{5,1},{2,6},{6,2},{3,7},{7,3},{8,12},{12,8},{9,1... | collective-permute-start | bytes 1179656 | tf_op jit(solution)/shard_map/ppermute | solution.py:40
  409.1 21.0 %collective-permute-start.106 = (f32[16,1024]{1,0:T(8,128)S(1)}, f32[16,1024]{1,0:T(8,128)}, u32[]{:S(2)}, u32[]{:S(2)}) collective-permute-start(f32[16,1024]{1,0:T(8,128)S(1)} %add.296), channel_id=1, source_target_pairs={{0,2},{1,3},{2,0},{3,1},{4,6},{5,7},{6,4},{7,5},{8,10},{9,11},{10,... | collective-permute-start | bytes 196616 | tf_op jit(solution)/shard_map/ppermute | solution.py:920
  430.1 64.7 %collective-permute-start.78 = (bf16[4,128,1280]{2,1,0:T(8,128)(2,1)}, bf16[4,128,1280]{2,1,0:T(8,128)(2,1)}, u32[]{:S(2)}, u32[]{:S(2)}) collective-permute-start(bf16[4,128,1280]{2,1,0:T(8,128)(2,1)} %get-tuple-element.171), channel_id=1, source_target_pairs={{0,16},{16,0},{1,17},{17,1},{2,18},{18,2},{3,19},{19,3},{4,20},{20... | collective-permute-start | bytes 3932168 | tf_op jit(solution)/shard_map/ppermute | solution.py:40
  430.8 47.5 %collective-permute-start.67 = (bf16[4,144,768]{2,1,0:T(8,128)(2,1)}, bf16[4,144,768]{2,1,0:T(8,128)(2,1)}, u32[]{:S(2)}, u32[]{:S(2)}) collective-permute-start(bf16[4,144,768]{2,1,0:T(8,128)(2,1)} %get-tuple-element.160), channel_id=1, source_target_pairs={{0,16},{16,0},{1,17},{17,1},{2,18},{18,2},{3,19},{19,3},{4,20},{20... | collective-permute-start | bytes 2654216 | tf_op jit(solution)/shard_map/ppermute | solution.py:40
  438.5 12.8 %collective-permute-start.91 = (bf16[128,2048]{1,0:T(8,128)(2,1)}, bf16[128,2048]{1,0:T(8,128)(2,1)S(1)}, u32[]{:S(2)}, u32[]{:S(2)}) collective-permute-start(bf16[128,2048]{1,0:T(8,128)(2,1)} %get-tuple-element.183), channel_id=1, source_target_pairs={{0,1},{1,2},{2,3},{3,0},{4,5},{5,6},{6,7},{7,4},{8,9},{9,10},{10,1... | collective-permute-start | bytes 1572872 | tf_op jit(solution)/shard_map/ppermute | solution.py:665
  438.6 44.2 %collective-permute-start.92 = (bf16[128,2048]{1,0:T(8,128)(2,1)}, bf16[128,2048]{1,0:T(8,128)(2,1)S(1)}, u32[]{:S(2)}, u32[]{:S(2)}) collective-permute-start(bf16[128,2048]{1,0:T(8,128)(2,1)} %get-tuple-element.184), channel_id=1, source_target_pairs={{0,2},{1,3},{2,0},{3,1},{4,6},{5,7},{6,4},{7,5},{8,10},{9,11},{10,... | collective-permute-start | bytes 1572872 | tf_op jit(solution)/shard_map/ppermute | solution.py:665
  439.6 50.1 %collective-permute-start.93 = (bf16[128,2048]{1,0:T(8,128)(2,1)}, bf16[128,2048]{1,0:T(8,128)(2,1)S(1)}, u32[]{:S(2)}, u32[]{:S(2)}) collective-permute-start(bf16[128,2048]{1,0:T(8,128)(2,1)} %get-tuple-element.185), channel_id=1, source_target_pairs={{0,3},{1,0},{2,1},{3,2},{4,7},{5,4},{6,5},{7,6},{8,11},{9,8},{10,9... | collective-permute-start | bytes 1572872 | tf_op jit(solution)/shard_map/ppermute | solution.py:665
  451.3 123.5 %collective-permute-start.65 = (bf16[672,1024]{1,0:T(8,128)(2,1)}, bf16[672,1024]{1,0:T(8,128)(2,1)}, u32[]{:S(2)}, u32[]{:S(2)}) collective-permute-start(bf16[672,1024]{1,0:T(8,128)(2,1)} %add_convert_fusion.1), channel_id=1, source_target_pairs={{0,8},{8,0},{1,9},{9,1},{2,10},{10,2},{3,11},{11,3},{4,12},{12,4},... | collective-permute-start | bytes 4128776 | tf_op jit(solution)/shard_map/ppermute | solution.py:40
  478.3 13.7 %collective-permute-start.62 = (bf16[3,32,1024]{2,1,0:T(8,128)(2,1)}, bf16[3,32,1024]{2,1,0:T(8,128)(2,1)S(1)}, u32[]{:S(2)}, u32[]{:S(2)}) collective-permute-start(bf16[3,32,1024]{2,1,0:T(8,128)(2,1)} %bitcast.22), channel_id=1, source_target_pairs={{0,0},{1,8},{2,4},{3,12},{4,2},{5,10},{6,6},{7,14},{8,1},{9,9},{10... | collective-permute-start | bytes 589832 | tf_op jit(solution)/shard_map/ppermute | solution.py:662
  482.8 17.9 %collective-permute-start.68 = (bf16[144,768]{1,0:T(8,128)(2,1)}, bf16[144,768]{1,0:T(8,128)(2,1)S(1)}, u32[]{:S(2)}, u32[]{:S(2)}) collective-permute-start(bf16[144,768]{1,0:T(8,128)(2,1)} %get-tuple-element.162), channel_id=1, source_target_pairs={{0,1},{1,2},{2,3},{3,0},{4,5},{5,6},{6,7},{7,4},{8,9},{9,10},{10,1... | collective-permute-start | bytes 663560 | tf_op jit(solution)/shard_map/ppermute | solution.py:665
  489.7 21.3 %collective-permute-start.69 = (bf16[144,768]{1,0:T(8,128)(2,1)}, bf16[144,768]{1,0:T(8,128)(2,1)S(1)}, u32[]{:S(2)}, u32[]{:S(2)}) collective-permute-start(bf16[144,768]{1,0:T(8,128)(2,1)} %get-tuple-element.163), channel_id=1, source_target_pairs={{0,2},{1,3},{2,0},{3,1},{4,6},{5,7},{6,4},{7,5},{8,10},{9,11},{10,... | collective-permute-start | bytes 663560 | tf_op jit(solution)/shard_map/ppermute | solution.py:665
  492.1 18.9 %collective-permute-start.70 = (bf16[144,768]{1,0:T(8,128)(2,1)}, bf16[144,768]{1,0:T(8,128)(2,1)S(1)}, u32[]{:S(2)}, u32[]{:S(2)}) collective-permute-start(bf16[144,768]{1,0:T(8,128)(2,1)} %get-tuple-element.164), channel_id=1, source_target_pairs={{0,3},{1,0},{2,1},{3,2},{4,7},{5,4},{6,5},{7,6},{8,11},{9,8},{10,9... | collective-permute-start | bytes 663560 | tf_op jit(solution)/shard_map/ppermute | solution.py:665
  494.8 35.1 %collective-permute-start.94 = (bf16[128,1024]{1,0:T(8,128)(2,1)}, bf16[128,1024]{1,0:T(8,128)(2,1)S(1)}, u32[]{:S(2)}, u32[]{:S(2)}) collective-permute-start(bf16[128,1024]{1,0:T(8,128)(2,1)} %get-tuple-element.187), channel_id=1, source_target_pairs={{0,0},{1,4},{2,8},{3,12},{4,16},{5,20},{6,24},{7,28},{8,1},{9,5},{... | collective-permute-start | bytes 786440 | tf_op jit(solution)/shard_map/ppermute | solution.py:794
  500.7 30.0 %collective-permute-start.79 = (bf16[128,1280]{1,0:T(8,128)(2,1)}, bf16[128,1280]{1,0:T(8,128)(2,1)S(1)}, u32[]{:S(2)}, u32[]{:S(2)}) collective-permute-start(bf16[128,1280]{1,0:T(8,128)(2,1)} %get-tuple-element.173), channel_id=1, source_target_pairs={{0,1},{1,2},{2,3},{3,0},{4,5},{5,6},{6,7},{7,4},{8,9},{9,10},{10,1... | collective-permute-start | bytes 983048 | tf_op jit(solution)/shard_map/ppermute | solution.py:665
  510.9 29.4 %collective-permute-start.80 = (bf16[128,1280]{1,0:T(8,128)(2,1)}, bf16[128,1280]{1,0:T(8,128)(2,1)}, u32[]{:S(2)}, u32[]{:S(2)}) collective-permute-start(bf16[128,1280]{1,0:T(8,128)(2,1)} %get-tuple-element.174), channel_id=1, source_target_pairs={{0,2},{1,3},{2,0},{3,1},{4,6},{5,7},{6,4},{7,5},{8,10},{9,11},{10,... | collective-permute-start | bytes 983048 | tf_op jit(solution)/shard_map/ppermute | solution.py:665
  510.9 40.0 %collective-permute-start.81 = (bf16[128,1280]{1,0:T(8,128)(2,1)}, bf16[128,1280]{1,0:T(8,128)(2,1)}, u32[]{:S(2)}, u32[]{:S(2)}) collective-permute-start(bf16[128,1280]{1,0:T(8,128)(2,1)} %get-tuple-element.175), channel_id=1, source_target_pairs={{0,3},{1,0},{2,1},{3,2},{4,7},{5,4},{6,5},{7,6},{8,11},{9,8},{10,9... | collective-permute-start | bytes 983048 | tf_op jit(solution)/shard_map/ppermute | solution.py:665
  529.9 23.3 %collective-permute-start.72 = (bf16[144,768]{1,0:T(8,128)(2,1)}, bf16[144,768]{1,0:T(8,128)(2,1)}, u32[]{:S(2)}, u32[]{:S(2)}) collective-permute-start(bf16[144,768]{1,0:T(8,128)(2,1)} %final_sum_kernel.3.refs_0_), channel_id=1, source_target_pairs={{0,8},{8,0},{1,9},{9,1},{2,10},{10,2},{3,11},{11,3},{4,12},{12,4},... | collective-permute-start | bytes 663560 | tf_op jit(solution)/shard_map/ppermute | solution.py:40
  530.7 41.6 %collective-permute-start.96 = (bf16[128,2048]{1,0:T(8,128)(2,1)S(1)}, bf16[128,2048]{1,0:T(8,128)(2,1)S(1)}, u32[]{:S(2)}, u32[]{:S(2)}) collective-permute-start(bf16[128,2048]{1,0:T(8,128)(2,1)S(1)} %constant_dynamic-update-slice_fusion.2.refs_0_), channel_id=1, source_target_pairs={{0,8},{8,0},{1,9},{9,1},{2,10},{10,2},{3,11},{11,3},{4,12},{12,4},... | collective-permute-start | bytes 1572872 | tf_op jit(solution)/shard_map/ppermute | solution.py:40
  540.3 33.5 %collective-permute-start.98 = (bf16[128,2048]{1,0:T(8,128)(2,1)S(1)}, bf16[128,2048]{1,0:T(8,128)(2,1)}, u32[]{:S(2)}, u32[]{:S(2)}) collective-permute-start(bf16[128,2048]{1,0:T(8,128)(2,1)S(1)} %constant_dynamic-update-slice_fusion.2.refs_0_), channel_id=1, source_target_pairs={{0,16},{16,0},{1,17},{17,1},{2,18},{18,2},{3,19},{19,3},{4,20},{20... | collective-permute-start | bytes 1572872 | tf_op jit(solution)/shard_map/ppermute | solution.py:40
  550.9 23.8 %collective-permute-start.95 = (bf16[128,2048]{1,0:T(8,128)(2,1)S(1)}, bf16[128,2048]{1,0:T(8,128)(2,1)}, u32[]{:S(2)}, u32[]{:S(2)}) collective-permute-start(bf16[128,2048]{1,0:T(8,128)(2,1)S(1)} %constant_dynamic-update-slice_fusion.2.refs_0_), channel_id=1, source_target_pairs={{0,4},{4,0},{1,5},{5,1},{2,6},{6,2},{3,7},{7,3},{8,12},{12,8},{9,1... | collective-permute-start | bytes 1572872 | tf_op jit(solution)/shard_map/ppermute | solution.py:40
  572.3 18.1 %collective-permute-start.100 = (bf16[128,2048]{1,0:T(8,128)(2,1)S(1)}, bf16[128,2048]{1,0:T(8,128)(2,1)}, u32[]{:S(2)}, u32[]{:S(2)}) collective-permute-start(bf16[128,2048]{1,0:T(8,128)(2,1)S(1)} %collective-permute-done.96.refs_2_), channel_id=1, source_target_pairs={{0,16},{16,0},{1,17},{17,1},{2,18},{18,2},{3,19},{19,3},{4,20},{20... | collective-permute-start | bytes 1572872 | tf_op jit(solution)/shard_map/ppermute | solution.py:40
  573.7 17.0 %collective-permute-start.97 = (bf16[128,2048]{1,0:T(8,128)(2,1)S(1)}, bf16[128,2048]{1,0:T(8,128)(2,1)S(1)}, u32[]{:S(2)}, u32[]{:S(2)}) collective-permute-start(bf16[128,2048]{1,0:T(8,128)(2,1)S(1)} %collective-permute-done.96.refs_2_), channel_id=1, source_target_pairs={{0,4},{4,0},{1,5},{5,1},{2,6},{6,2},{3,7},{7,3},{8,12},{12,8},{9,1... | collective-permute-start | bytes 1572872 | tf_op jit(solution)/shard_map/ppermute | solution.py:40
  574.7 18.8 %collective-permute-start.99 = (bf16[128,2048]{1,0:T(8,128)(2,1)}, bf16[128,2048]{1,0:T(8,128)(2,1)S(1)}, u32[]{:S(2)}, u32[]{:S(2)}) collective-permute-start(bf16[128,2048]{1,0:T(8,128)(2,1)} %collective-permute-done.98.refs_4_), channel_id=1, source_target_pairs={{0,4},{4,0},{1,5},{5,1},{2,6},{6,2},{3,7},{7,3},{8,12},{12,8},{9,1... | collective-permute-start | bytes 1572872 | tf_op jit(solution)/shard_map/ppermute | solution.py:40
  574.8 17.2 %collective-permute-start.84 = (bf16[128,1280]{1,0:T(8,128)(2,1)S(1)}, bf16[128,1280]{1,0:T(8,128)(2,1)S(1)}, u32[]{:S(2)}, u32[]{:S(2)}) collective-permute-start(bf16[128,1280]{1,0:T(8,128)(2,1)S(1)} %constant_dynamic-update-slice_fusion.refs_0_), channel_id=1, source_target_pairs={{0,8},{8,0},{1,9},{9,1},{2,10},{10,2},{3,11},{11,3},{4,12},{12,4},... | collective-permute-start | bytes 983048 | tf_op jit(solution)/shard_map/ppermute | solution.py:40
  579.1 52.1 %collective-permute-start.66 = (bf16[3,7,32,1024]{3,2,1,0:T(8,128)(2,1)}, bf16[3,7,32,1024]{3,2,1,0:T(8,128)(2,1)S(1)}, u32[]{:S(2)}, u32[]{:S(2)}) collective-permute-start(bf16[3,7,32,1024]{3,2,1,0:T(8,128)(2,1)} %bitcast.27), channel_id=1, source_target_pairs={{0,0},{1,8},{2,4},{3,12},{4,2},{5,10},{6,6},{7,14},{8,1},{9,9},{10... | collective-permute-start | bytes 4128776 | tf_op jit(solution)/shard_map/ppermute | solution.py:662
  592.0 13.5 %collective-permute-start.88 = (bf16[128,1280]{1,0:T(8,128)(2,1)S(1)}, bf16[128,1280]{1,0:T(8,128)(2,1)}, u32[]{:S(2)}, u32[]{:S(2)}) collective-permute-start(bf16[128,1280]{1,0:T(8,128)(2,1)S(1)} %collective-permute-done.84.refs_2_), channel_id=1, source_target_pairs={{0,16},{16,0},{1,17},{17,1},{2,18},{18,2},{3,19},{19,3},{4,20},{20... | collective-permute-start | bytes 983048 | tf_op jit(solution)/shard_map/ppermute | solution.py:40
  593.5 16.8 %collective-permute-start.101 = (bf16[128,2048]{1,0:T(8,128)(2,1)}, bf16[128,2048]{1,0:T(8,128)(2,1)S(1)}, u32[]{:S(2)}, u32[]{:S(2)}) collective-permute-start(bf16[128,2048]{1,0:T(8,128)(2,1)} %collective-permute-done.100.refs_6_), channel_id=1, source_target_pairs={{0,4},{4,0},{1,5},{5,1},{2,6},{6,2},{3,7},{7,3},{8,12},{12,8},{9,1... | collective-permute-start | bytes 1572872 | tf_op jit(solution)/shard_map/ppermute | solution.py:40
  609.8 14.7 %collective-permute-start.71 = (bf16[144,768]{1,0:T(8,128)(2,1)S(1)}, bf16[144,768]{1,0:T(8,128)(2,1)S(1)}, u32[]{:S(2)}, u32[]{:S(2)}) collective-permute-start(bf16[144,768]{1,0:T(8,128)(2,1)S(1)} %copy-done.12), channel_id=1, source_target_pairs={{0,4},{4,0},{1,5},{5,1},{2,6},{6,2},{3,7},{7,3},{8,12},{12,8},{9,1... | collective-permute-start | bytes 663560 | tf_op jit(solution)/shard_map/ppermute | solution.py:40
  609.8 14.7 %collective-permute-start.73 = (bf16[144,768]{1,0:T(8,128)(2,1)}, bf16[144,768]{1,0:T(8,128)(2,1)S(1)}, u32[]{:S(2)}, u32[]{:S(2)}) collective-permute-start(bf16[144,768]{1,0:T(8,128)(2,1)} %collective-permute-done.72.refs_2_), channel_id=1, source_target_pairs={{0,4},{4,0},{1,5},{5,1},{2,6},{6,2},{3,7},{7,3},{8,12},{12,8},{9,1... | collective-permute-start | bytes 663560 | tf_op jit(solution)/shard_map/ppermute | solution.py:40
  610.3 14.2 %collective-permute-start.75 = (bf16[144,768]{1,0:T(8,128)(2,1)}, bf16[144,768]{1,0:T(8,128)(2,1)S(1)}, u32[]{:S(2)}, u32[]{:S(2)}) collective-permute-start(bf16[144,768]{1,0:T(8,128)(2,1)} %copy-done.68), channel_id=1, source_target_pairs={{0,4},{4,0},{1,5},{5,1},{2,6},{6,2},{3,7},{7,3},{8,12},{12,8},{9,1... | collective-permute-start | bytes 663560 | tf_op jit(solution)/shard_map/ppermute | solution.py:40
  610.4 14.2 %collective-permute-start.77 = (bf16[144,768]{1,0:T(8,128)(2,1)}, bf16[144,768]{1,0:T(8,128)(2,1)}, u32[]{:S(2)}, u32[]{:S(2)}) collective-permute-start(bf16[144,768]{1,0:T(8,128)(2,1)} %copy-done.69), channel_id=1, source_target_pairs={{0,4},{4,0},{1,5},{5,1},{2,6},{6,2},{3,7},{7,3},{8,12},{12,8},{9,1... | collective-permute-start | bytes 663560 | tf_op jit(solution)/shard_map/ppermute | solution.py:40
  (146 other events, 2089.7 us)
